TPU v7x, 256 devices: a whole 4x4x8 slice. The times are simulated.
256 devices in a mesh: cluster: 8 (over x, core), coupling: 32 (over z, y).
Axes of the slice: x: 4, y: 4, z: 8, core: 2. Of those that a mesh axis runs over, the one named last changes fastest.
Arguments:
- charges: bfloat16 [16384, 64, 64], P(('cluster', 'coupling')), may hold values from -6 to 6
- source_basis: bfloat16 [16384, 64, 64], P(('cluster', 'coupling')), may hold values from -0.75 to 0.75
- target_basis: bfloat16 [16384, 64, 64], P(('cluster', 'coupling')), may hold values from -0.75 to 0.75
- leaf_up: bfloat16 [16384, 64, 64], P(('cluster', 'coupling')), may hold values from -0.25 to 0.25
- mid_up: bfloat16 [2048, 64, 64], P(('cluster', 'coupling')), may hold values from -0.25 to 0.25
- leaf_down: bfloat16 [16384, 64, 64], P(('cluster', 'coupling')), may hold values from -0.75 to 0.75
- mid_down: bfloat16 [2048, 64, 64], P(('cluster', 'coupling')), may hold values from -0.75 to 0.75
- leaf_far_src: int32 [16384, 8], P(('cluster', 'coupling')), may hold values from 0 to 16383, as said below
- leaf_far_mat: bfloat16 [16384, 8, 64, 64], P(('cluster', 'coupling')), may hold values from -0.25 to 0.25
- mid_far_src: int32 [2048, 16], P(('cluster', 'coupling')), may hold values from 0 to 2047, as said below
- mid_far_mat: bfloat16 [2048, 16, 64, 64], P(('cluster', 'coupling')), may hold values from -0.1875 to 0.1875
- top_far_src: int32 [256, 32], P(('cluster', 'coupling')), may hold values from 0 to 255
- top_far_mat: bfloat16 [256, 32, 64, 64], P(('cluster', 'coupling')), may hold values from -0.125 to 0.125
- near_src: int32 [16384, 8], P(('cluster', 'coupling')), may hold values from 0 to 16383, as said below
- near_count: int32 [16384], P(('cluster', 'coupling')), may hold values from 1 to 8, as said below
- near_mat: bfloat16 [16384, 8, 64, 64], P(('cluster', 'coupling')), may hold values from -0.25 to 0.25
Outputs:
- potential: bfloat16 [16384, 64, 64], P(('cluster', 'coupling'))
Inputs may be any that keep to these rules, and one draw needn't show every extreme that they name: `leaf_far_src`: the sources of a leaf's coupling entries lie on the leaf's own device or on the devices just before or after it in the order cluster+coupling; entry 0 lies on the device before and entry 1 on the device after, where those exist. `near_src`: the sources of a leaf's near-field slots lie on the leaf's own device or on the devices just before or after it in the order cluster+coupling; slot 0 lies on the device before and slot 1 on the device after, where those exist. Only the first near_count[l] slots of leaf l are used. `mid_far_src`: the sources of a level-1 cluster p lie in its own block of 256 level-1 clusters, p // 256.
All inputs are finite; a program needn't handle non-finite values.
Results may differ from a plain program's by a relative error of at most 0.012.
Values may be sent and summed in bfloat16 or wider, within the bound.
No kernel may reach another device: no remote copies, remote signals or barrier semaphores. Data moves between devices by JAX's collectives and lax.ppermute only.
A program may use at most 128 MiB of HBM per device.

v0:
```python
import jax
import jax.numpy as jnp
from jax import lax
from jax.sharding import PartitionSpec as P


def with_halo(x, sides, width):
    for axis, dim in sides:
        size, length = (lax.axis_size(axis), x.shape[dim])
        up = [(i, (i + 1) % size) for i in range(size - 1)]
        down = [(j, i) for i, j in up]
        last = lax.slice_in_dim(x, length - width, length, axis=dim)
        initial = lax.slice_in_dim(x, 0, width, axis=dim)
        before = lax.ppermute(last, axis, up)
        after = lax.ppermute(initial, axis, down)
        x = jnp.concatenate([before, x, after], axis=dim)
    return x


def product(form, left, right):
    return jnp.einsum(form, left, right, preferred_element_type=jnp.float32)


def shards(
    charges,
    source_basis,
    target_basis,
    leaf_up,
    mid_up,
    leaf_down,
    mid_down,
    leaf_far_src,
    leaf_far_mat,
    mid_far_src,
    mid_far_mat,
    top_far_src,
    top_far_mat,
    near_src,
    near_count,
    near_mat,
):
    leaf_rows = charges.shape[0]
    rank_size = source_basis.shape[2]
    columns = charges.shape[2]
    device = lax.axis_index(("cluster", "coupling"))
    offset_rows = (device - 1) * leaf_rows
    leaf_coef = product("lpk,lpr->lkr", source_basis, charges).astype(jnp.bfloat16)
    near_used = (lax.broadcasted_iota(jnp.int32, near_src.shape, 1) < near_count[:, None]).astype(
        jnp.bfloat16
    )
    near_local = near_src - offset_rows
    far_local = leaf_far_src - offset_rows
    padded_charges = with_halo(charges, ((("cluster", "coupling"), 0),), leaf_rows)
    picked = padded_charges[near_local] * near_used[:, :, None, None]
    near_term = product("lnpq,lnqr->lpr", near_mat, picked)
    padded_coef = with_halo(leaf_coef, ((("cluster", "coupling"), 0),), leaf_rows)
    mid_coef = (
        product("lkj,lkr->ljr", leaf_up, leaf_coef)
        .reshape(leaf_rows // 8, 8, rank_size, columns)
        .sum(axis=1)
        .astype(jnp.bfloat16)
    )
    top_coef = (
        product("pkj,pkr->pjr", mid_up, mid_coef)
        .reshape(leaf_rows // 64, 8, rank_size, columns)
        .sum(axis=1)
        .astype(jnp.bfloat16)
    )
    all_top = lax.all_gather(top_coef, ("cluster", "coupling"), axis=0, tiled=True)
    top_local = product("gnjk,gnkr->gjr", top_far_mat, all_top[top_far_src]).astype(jnp.bfloat16)
    mid_count = mid_coef.shape[0]
    row_begin = lax.axis_index("cluster") * (mid_count * lax.axis_size("coupling"))
    mid_index = mid_far_src - row_begin
    row_coef = lax.all_gather(mid_coef, "coupling", axis=0, tiled=True)
    selected = row_coef[mid_index]
    mid_far = product("pnjk,pnkr->pjr", mid_far_mat, selected)
    mid_local = (
        mid_far + product("pkj,pjr->pkr", mid_down, jnp.repeat(top_local, 8, axis=0))
    ).astype(jnp.bfloat16)
    leaf_far = product("lnjk,lnkr->ljr", leaf_far_mat, padded_coef[far_local])
    leaf_local = (
        leaf_far + product("lkj,ljr->lkr", leaf_down, jnp.repeat(mid_local, 8, axis=0))
    ).astype(jnp.bfloat16)
    return (product("lpk,lkr->lpr", target_basis, leaf_local) + near_term).astype(jnp.bfloat16)


def solution(mesh):
    in_specs = (
        P(("cluster", "coupling"), None, None),
        P(("cluster", "coupling"), None, None),
        P(("cluster", "coupling"), None, None),
        P(("cluster", "coupling"), None, None),
        P(("cluster", "coupling"), None, None),
        P(("cluster", "coupling"), None, None),
        P(("cluster", "coupling"), None, None),
        P(("cluster", "coupling"), None),
        P(("cluster", "coupling"), None, None, None),
        P(("cluster", "coupling"), None),
        P(("cluster", "coupling"), None, None, None),
        P(("cluster", "coupling"), None),
        P(("cluster", "coupling"), None, None, None),
        P(("cluster", "coupling"), None),
        P(("cluster", "coupling")),
        P(("cluster", "coupling"), None, None, None),
    )
    out_specs = P(("cluster", "coupling"), None, None)
    return jax.shard_map(shards, mesh=mesh, in_specs=in_specs, out_specs=out_specs, check_vma=False)
```

profile of v0, /device:TPU:1, one launch (start us, length us, event | category | flops | bytes accessed | tf_op | source)
XLA Modules:
  0.0 274.8 jit_solution(13306328828408738497)
XLA Ops:
  6.6 2.2 convolution_convert_fusion
  8.8 0.5 bitcast_reduce_fusion
  9.4 0.8 copy.47
  10.4 0.7 copy.49
  11.2 4.0 %collective-permute-start = (bf16[64,64,64]{2,1,0:T(8,128)(2,1)S(1)}, bf16[64,64,64]{2,1,0:T(8,128)(2,1)}, u32[]{:S(2)}, u32[]{:S(2)}) collective-permute-start(bf16[64,64,64]{2,1,0:T(8,128)(2,1)S(1)} %convolution_convert_fusion), channel_id=1, source_target_pairs={{0,1},{1,2},{2,3},{3,4},{4,5},{5,6},{6,7},{7,8},{8,9},{9,10},{10,1... | collective-permute-start | bytes 1572872 | tf_op jit(solution)/shard_map/ppermute | solution.py:14
  15.2 9.2 %collective-permute-start.1 = (bf16[64,64,64]{2,1,0:T(8,128)(2,1)S(1)}, bf16[64,64,64]{2,1,0:T(8,128)(2,1)}, u32[]{:S(2)}, u32[]{:S(2)}) collective-permute-start(bf16[64,64,64]{2,1,0:T(8,128)(2,1)S(1)} %convolution_convert_fusion), channel_id=1, source_target_pairs={{1,0},{2,1},{3,2},{4,3},{5,4},{6,5},{7,6},{8,7},{9,8},{10,9},{11,1... | collective-permute-start | bytes 1572872 | tf_op jit(solution)/shard_map/ppermute | solution.py:15
  24.4 1.9 collective-permute-start.2
  26.4 7.0 %collective-permute-start.3 = (bf16[64,64,64]{2,1,0:T(8,128)(2,1)}, bf16[64,64,64]{2,1,0:T(8,128)(2,1)}, u32[]{:S(2)}, u32[]{:S(2)}) collective-permute-start(bf16[64,64,64]{2,1,0:T(8,128)(2,1)} %param.16), channel_id=1, source_target_pairs={{1,0},{2,1},{3,2},{4,3},{5,4},{6,5},{7,6},{8,7},{9,8},{10,9},{11,1... | collective-permute-start | bytes 1572872 | tf_op jit(solution)/shard_map/ppermute | solution.py:15
  33.9 0.6 pad_clamp_fusion.1
  34.6 34.1 %collective-permute-done.2 = bf16[64,64,64]{2,1,0:T(8,128)(2,1)} collective-permute-done((bf16[64,64,64]{2,1,0:T(8,128)(2,1)}, bf16[64,64,64]{2,1,0:T(8,128)(2,1)}, u32[]{:S(2)}, u32[]{:S(2)}) %collective-permute-start.2) | collective-permute-done | bytes 524320 | tf_op jit(solution)/shard_map/ppermute | solution.py:14
  68.6 3.4 %pad_maximum_fusion.1 = bf16[192,64,64]{2,1,0:T(8,128)(2,1)} fusion(bf16[64,64,64]{2,1,0:T(8,128)(2,1)} %collective-permute-done.3, bf16[64,64,64]{2,1,0:T(8,128)(2,1)} %param.16, bf16[64,64,64]{2,1,0:T(8,128)(2,1)} %collective-permute-done.2), kind=kLoop, calls=%fused_computation.8 | loop fusion | flops 1572864 | bytes 3145728 | tf_op jit(solution)/shard_map/concatenate | solution.py:16
  72.1 21.5 %gather_fusion.3 = bf16[512,64,64]{2,1,0:T(8,128)(2,1)} fusion(bf16[192,64,64]{2,1,0:T(8,128)(2,1)} %pad_maximum_fusion.1, s32[1024]{0:T(1024)S(1)} %pad_clamp_fusion), kind=kCustom, calls=%fused_computation.3 | custom fusion | bytes 8390656 | tf_op jit(solution)/shard_map/gather | solution.py:54
  93.6 12.0 %copy.54 = bf16[64,8,64,64]{2,3,1,0:T(8,128)(2,1)} copy(bf16[64,8,64,64]{3,2,1,0:T(8,128)(2,1)} %bitcast.68) | data formatting | bytes 8388608 | tf_op jit(solution)/shard_map/gather | solution.py:54
  105.6 3.3 %pad_maximum_fusion = bf16[192,64,64]{2,1,0:T(8,128)(2,1)} fusion(bf16[64,64,64]{2,1,0:T(8,128)(2,1)} %collective-permute-done.1, bf16[64,64,64]{2,1,0:T(8,128)(2,1)S(1)} %convolution_convert_fusion, bf16[64,64,64]{2,1,0:T(8,128)(2,1)} %collective-permute-done), kind=kLoop, calls=%fused_computation.7 | loop fusion | flops 1572864 | bytes 3145728 | tf_op jit(solution)/shard_map/concatenate | solution.py:16
  108.9 21.8 %gather_fusion = bf16[512,64,64]{2,1,0:T(8,128)(2,1)} fusion(bf16[192,64,64]{2,1,0:T(8,128)(2,1)} %pad_maximum_fusion, s32[1024]{0:T(1024)S(1)} %pad_clamp_fusion.3), kind=kCustom, calls=%fused_computation | custom fusion | bytes 8390656 | tf_op jit(solution)/shard_map/gather | solution.py:80
  130.7 4.4 %gather_fusion.1 = bf16[128,64,64]{2,1,0:T(8,128)(2,1)} fusion(bf16[256,64,64]{2,1,0:T(8,128)(2,1)} %all-gather.4.cloned.1.call-done, s32[1024]{0:T(1024)S(1)} %pad_clamp_fusion.2), kind=kCustom, calls=%fused_computation.1 | custom fusion | bytes 2097664 | tf_op jit(solution)/shard_map/gather | solution.py:75
  135.1 2.5 convolution_bitcast_fusion
  137.6 105.1 %all-gather.6.cloned.1.call-done = bf16[16384,64]{1,0:T(8,128)(2,1)} async-done(((bf16[64,64]{1,0:T(8,128)(2,1)}), bf16[16384,64]{1,0:T(8,128)(2,1)}) %all-gather.6.cloned.1.call-update) | async-done | bytes 2097168 | tf_op jit(solution)/shard_map/all_gather | solution.py:69
  242.7 3.0 %gather_fusion.2 = bf16[32,64,64]{2,1,0:T(8,128)(2,1)S(1)} fusion(bf16[256,64,64]{2,1,0:T(8,128)(2,1)} %bitcast.71, s32[1024]{0:T(1024)} %pad_clamp_fusion.1), kind=kCustom, calls=%fused_computation.2 | custom fusion | bytes 524416 | tf_op jit(solution)/shard_map/gather | solution.py:70
  245.6 1.4 fusion.15
  247.5 0.7 fusion.21
  248.2 10.3 %fusion.7 = f32[64,64,64]{2,1,0:T(8,128)} fusion(bf16[64,64,64]{2,1,0:T(8,128)(2,1)} %param.18, f32[64,64,64]{2,1,0:T(8,128)S(1)} %fusion.21, bf16[64,8,64,64]{3,2,1,0:T(8,128)(2,1)} %bitcast.67, bf16[64,8,64,64]{3,2,1,0:T(8,128)(2,1)} %param.24), kind=kOutput, calls=%fused_computation.15 | convolution fusion | flops 302514176 | bytes 11010048 | tf_op jit(solution)/shard_map/lpk,lkr->lpr/dot_general | solution.py:21
  258.4 8.2 %fusion.8 = bf16[64,64,64]{1,2,0:T(8,128)(2,1)S(1)} fusion(f32[64,64,64]{2,1,0:T(8,128)} %fusion.7, bf16[64,8,64,64]{3,2,1,0:T(8,128)(2,1)} %param.31, bf16[64,8,64,64]{2,3,1,0:T(8,128)(2,1)} %copy.54, bf16[64,8]{1,0:T(8,128)(2,1)S(1)} %fusion.19), kind=kOutput, calls=%fused_computation.16 | convolution fusion | flops 271056896 | bytes 9962496 | tf_op jit(solution)/shard_map/lnpq,lnqr->lpr/dot_general | solution.py:21
  266.6 1.3 copy.55
  (45 shorter events, 1.4 us)
Async XLA Ops:
  6.5 128.6 %copy-start = (bf16[8,16,64,64]{3,2,1,0:T(8,128)(2,1)S(1)}, bf16[8,16,64,64]{3,2,1,0:T(8,128)(2,1)}, u32[]{:S(2)}) copy-start(bf16[8,16,64,64]{3,2,1,0:T(8,128)(2,1)} %param.26) | copy-start | bytes 3145732
  6.5 3.7 %copy-start.4 = (bf16[8,64,64]{2,1,0:T(8,128)(2,1)S(1)}, bf16[8,64,64]{2,1,0:T(8,128)(2,1)}, u32[]{:S(2)}) copy-start(bf16[8,64,64]{2,1,0:T(8,128)(2,1)} %param.20) | copy-start | bytes 196612
  6.5 26.8 %copy-start.8 = (s32[64,8]{0,1:T(8,128)S(1)}, s32[64,8]{0,1:T(8,128)}, u32[]{:S(2)}) copy-start(s32[64,8]{0,1:T(8,128)} %param.23) | copy-start | bytes 6148
  6.5 26.8 %copy-start.7 = (s32[64,8]{0,1:T(8,128)S(1)}, s32[64,8]{0,1:T(8,128)}, u32[]{:S(2)}) copy-start(s32[64,8]{0,1:T(8,128)} %param.29) | copy-start | bytes 6148
  6.5 27.0 %copy-start.6 = (s32[8,16]{1,0:T(8,128)S(1)}, s32[8,16]{1,0:T(8,128)}, u32[]{:S(2)}) copy-start(s32[8,16]{1,0:T(8,128)} %param.25) | copy-start | bytes 1540
  6.5 27.3 %copy-start.10 = (s32[1,32]{1,0:T(1,128)S(1)}, s32[1,32]{1,0:T(1,128)}, u32[]{:S(2)}) copy-start(s32[1,32]{1,0:T(1,128)} %param.27) | copy-start | bytes 388
  6.6 27.9 %copy-start.9 = (s32[64]{0:T(128)S(1)}, s32[64]{0:T(128)}, u32[]{:S(2)}) copy-start(s32[64]{0:T(128)} %param.30) | copy-start | bytes 772
  6.6 124.1 %all-gather.4.cloned.1.call-start = ((), (), s32[]{:S(2)}) async-start(), calls=%async_computation | async-start | bytes 4325376 | tf_op jit(solution)/shard_map/all_gather | solution.py:74
  6.6 2.2 copy-start.2
  10.2 232.5 %all-gather.6.cloned.1.call-start = ((), (), s32[]{:S(2)}) async-start(), calls=%async_computation.1 | async-start | bytes 4210688 | tf_op jit(solution)/shard_map/all_gather | solution.py:69
  11.2 94.4 %collective-permute-start = (bf16[64,64,64]{2,1,0:T(8,128)(2,1)S(1)}, bf16[64,64,64]{2,1,0:T(8,128)(2,1)}, u32[]{:S(2)}, u32[]{:S(2)}) collective-permute-start(bf16[64,64,64]{2,1,0:T(8,128)(2,1)S(1)} %convolution_convert_fusion), channel_id=1, source_target_pairs={{0,1},{1,2},{2,3},{3,4},{4,5},{5,6},{6,7},{7,8},{8,9},{9,10},{10,1... | collective-permute-start | bytes 1572872 | tf_op jit(solution)/shard_map/ppermute | solution.py:14
  15.2 90.4 %collective-permute-start.1 = (bf16[64,64,64]{2,1,0:T(8,128)(2,1)S(1)}, bf16[64,64,64]{2,1,0:T(8,128)(2,1)}, u32[]{:S(2)}, u32[]{:S(2)}) collective-permute-start(bf16[64,64,64]{2,1,0:T(8,128)(2,1)S(1)} %convolution_convert_fusion), channel_id=1, source_target_pairs={{1,0},{2,1},{3,2},{4,3},{5,4},{6,5},{7,6},{8,7},{9,8},{10,9},{11,1... | collective-permute-start | bytes 1572872 | tf_op jit(solution)/shard_map/ppermute | solution.py:15
  24.4 44.2 %collective-permute-start.2 = (bf16[64,64,64]{2,1,0:T(8,128)(2,1)}, bf16[64,64,64]{2,1,0:T(8,128)(2,1)}, u32[]{:S(2)}, u32[]{:S(2)}) collective-permute-start(bf16[64,64,64]{2,1,0:T(8,128)(2,1)} %param.16), channel_id=1, source_target_pairs={{0,1},{1,2},{2,3},{3,4},{4,5},{5,6},{6,7},{7,8},{8,9},{9,10},{10,1... | collective-permute-start | bytes 1572872 | tf_op jit(solution)/shard_map/ppermute | solution.py:14
  26.4 42.3 %collective-permute-start.3 = (bf16[64,64,64]{2,1,0:T(8,128)(2,1)}, bf16[64,64,64]{2,1,0:T(8,128)(2,1)}, u32[]{:S(2)}, u32[]{:S(2)}) collective-permute-start(bf16[64,64,64]{2,1,0:T(8,128)(2,1)} %param.16), channel_id=1, source_target_pairs={{1,0},{2,1},{3,2},{4,3},{5,4},{6,5},{7,6},{8,7},{9,8},{10,9},{11,1... | collective-permute-start | bytes 1572872 | tf_op jit(solution)/shard_map/ppermute | solution.py:15
  135.1 111.9 %copy-start.5 = (bf16[8,64,64]{2,1,0:T(8,128)(2,1)S(1)}, bf16[8,64,64]{2,1,0:T(8,128)(2,1)}, u32[]{:S(2)}) copy-start(bf16[8,64,64]{2,1,0:T(8,128)(2,1)} %param.22) | copy-start | bytes 196612
  135.1 112.4 %copy-start.3 = (bf16[64,64,64]{2,1,0:T(8,128)(2,1)S(1)}, bf16[64,64,64]{2,1,0:T(8,128)(2,1)}, u32[]{:S(2)}) copy-start(bf16[64,64,64]{2,1,0:T(8,128)(2,1)} %param.21) | copy-start | bytes 1572868
  258.4 9.5 %copy-start.1 = (bf16[8,16,64,64]{3,2,1,0:T(8,128)(2,1)S(1)}, bf16[8,16,64,64]{3,2,1,0:T(8,128)(2,1)}, u32[]{:S(2)}) copy-start(bf16[8,16,64,64]{3,2,1,0:T(8,128)(2,1)} %param.26) | copy-start | bytes 3145732
Sparse Core Ops, SparseCore 0:
  10.3 113.0 all-gather.3
  127.1 115.4 all-gather.5
where the time goes:
time: 275 us
  waiting for transfers between devices  139 us (51%)
  local copies, waits for them, and re-layouts  66.2 us (24%)
  matrix products  26.1 us (9%)
  starting transfers between devices  22.2 us (8%)
  between operations  13.7 us (5%)
  other arithmetic  7.41 us (3%)
    all_gather x1, waiting for transfers between devices, shards(): lax.all_gather(top_coef, ('cluster', 'coupling'), axis=0, tiled=True)  105 us
    ppermute x2, waiting for transfers between devices, with_halo(): before = lax.ppermute(last, axis, up)  34.1 us
    gather x2, local copies, waits for them, and re-layouts, shards(): picked = padded_charges[near_local] * near_used[:, :, None, None]  33.5 us
    dot_general x9, matrix products, product(): return jnp.einsum(form, left, right, preferred_element_type=jnp.float32)  26.1 us
    gather x1, local copies, waits for them, and re-layouts, shards(): leaf_far = product('lnjk,lnkr->ljr', leaf_far_mat, padded_coef[far_local])  21.8 us
    ppermute x2, starting transfers between devices, with_halo(): after = lax.ppermute(initial, axis, down)  16.2 us
    concatenate x2, other arithmetic, with_halo(): x = jnp.concatenate([before, x, after], axis=dim)  6.72 us
    ppermute x2, starting transfers between devices, with_halo(): before = lax.ppermute(last, axis, up)  5.96 us
  transfers between devices with their start and end apart: 6, of which 2 were waited for; matrix products, arithmetic and copies ran while one was open for 26% of the time, Pallas kernels for 0%

commit v1 on v0

v1 whole, which is shorter than its diff:
```python
import functools

import jax
import jax.numpy as jnp
from jax import lax
from jax.experimental import pallas as pl
from jax.experimental.pallas import tpu as pltpu
from jax.sharding import PartitionSpec as P

BOTH = ("cluster", "coupling")
X, CORE, Z, Y = 4, 2, 8, 4
R = 64
BF = jnp.bfloat16
F32 = jnp.float32
VMEM = pltpu.VMEM


def dot(a, b):
    return lax.dot_general(a, b, (((1,), (0,)), ((), ())), preferred_element_type=F32)


def dot_t(a, b):
    return lax.dot_general(a, b, (((0,), (0,)), ((), ())), preferred_element_type=F32)


def beside(a, b):
    return jnp.concatenate([a, b], axis=1)


def wide(blocks):
    return jnp.concatenate([beside(a, b) for a, b in zip(blocks[::2], blocks[1::2])], axis=1)


def up_kernel(c_ref, s_ref, lu_ref, mu_ref, pc_ref, pk_ref, mt_ref, acc):
    i = pl.program_id(0)

    @pl.when(i == 0)
    def _():
        acc[...] = jnp.zeros_like(acc)

    coefs = []
    for l in range(16):
        coefs.append(dot_t(s_ref[l], c_ref[l]).astype(BF))
    for j in range(8):
        pc_ref[j] = beside(c_ref[2 * j], c_ref[2 * j + 1])
        pk_ref[j] = beside(coefs[2 * j], coefs[2 * j + 1])
    mids = []
    for h in range(2):
        up = lu_ref[8 * h : 8 * h + 8].reshape(8 * R, R)
        mids.append(dot_t(up, jnp.concatenate(coefs[8 * h : 8 * h + 8], axis=0)).astype(BF))
    mt_ref[pl.ds(pl.multiple_of(i * R, R), R), :] = beside(*mids)
    acc[...] += dot_t(mu_ref[...].reshape(2 * R, R), jnp.concatenate(mids, axis=0))

    @pl.when(i == 3)
    def _():
        top = acc[...].astype(BF)
        mt_ref[256:288, :] = beside(top[:32], top[32:])


def upsweep(charges, source_basis, leaf_up, mid_up):
    leaf = pl.BlockSpec((16, R, R), lambda i: (i, 0, 0))
    pair = pl.BlockSpec((8, R, 2 * R), lambda i: (i, 0, 0))
    return pl.pallas_call(
        up_kernel,
        grid=(4,),
        in_specs=[leaf, leaf, leaf, pl.BlockSpec((2, R, R), lambda i: (i, 0, 0))],
        out_specs=[pair, pair, pl.BlockSpec((288, 128), lambda i: (0, 0))],
        out_shape=[
            jax.ShapeDtypeStruct((32, R, 2 * R), BF),
            jax.ShapeDtypeStruct((32, R, 2 * R), BF),
            jax.ShapeDtypeStruct((288, 128), BF),
        ],
        scratch_shapes=[VMEM((R, R), F32)],
        compiler_params=pltpu.CompilerParams(vmem_limit_bytes=16 << 20),
        cost_estimate=pl.CostEstimate(flops=136 * 2 * R**3, bytes_accessed=5 << 20, transcendentals=0),
        name="upsweep",
    )(charges, source_basis, leaf_up, mid_up)


def unpack(table, refs):
    def step(j, carry):
        for b, ref in enumerate(refs):
            x = ref[j]
            table[64 * b + 2 * j] = x[:, :R]
            table[64 * b + 2 * j + 1] = x[:, R:]
        return carry

    lax.fori_loop(0, 32, step, 0)


def near_kernel(info, src, cnt, bef, own, aft, mat, out, table):
    i = pl.program_id(0)

    @pl.when(i == 0)
    def _():
        unpack(table, (bef, own, aft))
        table[192] = jnp.zeros((R, R), BF)

    for j in range(8):
        l = i * 8 + j
        rows = []
        for n in range(8):
            k = jnp.clip(src[n, l] - info[0], 0, 191)
            rows.append(table[jnp.where(n < cnt[l], k, 192)])
        acc = dot(wide([mat[j, n] for n in range(4)]), jnp.concatenate(rows[:4], axis=0))
        out[j] = acc + dot(wide([mat[j, n] for n in range(4, 8)]), jnp.concatenate(rows[4:], axis=0))


def near_field(info, src, cnt, bef, own, aft, mat):
    whole = pl.BlockSpec((32, R, 2 * R), lambda i, *_: (0, 0, 0))
    return pl.pallas_call(
        near_kernel,
        grid_spec=pltpu.PrefetchScalarGridSpec(
            num_scalar_prefetch=3,
            grid=(8,),
            in_specs=[whole, whole, whole, pl.BlockSpec((8, 8, R, R), lambda i, *_: (i, 0, 0, 0))],
            out_specs=pl.BlockSpec((8, R, R), lambda i, *_: (i, 0, 0)),
            scratch_shapes=[VMEM((193, R, R), BF)],
        ),
        out_shape=jax.ShapeDtypeStruct((64, R, R), F32),
        compiler_params=pltpu.CompilerParams(vmem_limit_bytes=24 << 20),
        cost_estimate=pl.CostEstimate(flops=512 * 2 * R**3, bytes_accessed=12 << 20, transcendentals=0),
        name="near",
    )(info, src, cnt, bef, own, aft, mat)


def far_kernel(info, src, bef, own, aft, mat, tb, ld, near, base, both, table):
    i = pl.program_id(0)

    @pl.when(i == 0)
    def _():
        unpack(table, (bef, own, aft))

    for j in range(8):
        l = i * 8 + j
        rows = [table[jnp.clip(src[n, l] - info[0], 0, 191)] for n in range(8)]
        acc = dot(wide([mat[j, n] for n in range(4)]), jnp.concatenate(rows[:4], axis=0))
        acc += dot(wide([mat[j, n] for n in range(4, 8)]), jnp.concatenate(rows[4:], axis=0))
        t = tb[j]
        base[j] = near[j] + dot(t, acc.astype(BF))
        both[j] = dot(t, ld[j]).astype(BF)


def leaf_far(info, src, bef, own, aft, mat, tb, ld, near):
    whole = pl.BlockSpec((32, R, 2 * R), lambda i, *_: (0, 0, 0))
    leaf = pl.BlockSpec((8, R, R), lambda i, *_: (i, 0, 0))
    return pl.pallas_call(
        far_kernel,
        grid_spec=pltpu.PrefetchScalarGridSpec(
            num_scalar_prefetch=2,
            grid=(8,),
            in_specs=[whole, whole, whole, pl.BlockSpec((8, 8, R, R), lambda i, *_: (i, 0, 0, 0)), leaf, leaf, leaf],
            out_specs=[leaf, leaf],
            scratch_shapes=[VMEM((192, R, R), BF)],
        ),
        out_shape=[jax.ShapeDtypeStruct((64, R, R), F32), jax.ShapeDtypeStruct((64, R, R), BF)],
        compiler_params=pltpu.CompilerParams(vmem_limit_bytes=24 << 20),
        cost_estimate=pl.CostEstimate(flops=640 * 2 * R**3, bytes_accessed=16 << 20, transcendentals=0),
        name="leaf_far",
    )(info, src, bef, own, aft, mat, tb, ld, near)


def top_kernel(info, src, own, other, mat, out):
    x, core, z, y = info[1], info[2], info[3], info[4]
    acc = jnp.zeros((R, R), F32)
    rows = []
    for n in range(32):
        g = jnp.clip(src[0, n], 0, X * CORE * Z * Y - 1)
        sy = lax.rem(y - lax.rem(g, Y) + Y, Y)
        sz = lax.rem(z - lax.rem(g // Y, Z) + Z, Z)
        sx = lax.rem(x - g // (CORE * Z * Y) + X, X)
        same = lax.rem(g // (Z * Y), CORE) == core
        at = pl.ds(pl.multiple_of(((sx * Z + sz) * Y + sy) * 32, 32), 32)
        t = jnp.where(same, own[at, :], other[at, :])
        rows += [t[:, :R], t[:, R:]]
    for q in range(8):
        acc += dot(wide([mat[0, 4 * q + n] for n in range(4)]), jnp.concatenate(rows[8 * q : 8 * q + 8], axis=0))
    out[...] = acc.astype(BF)


def top_far(info, src, own, other, mat):
    v = pl.BlockSpec(memory_space=VMEM)
    s = pl.BlockSpec(memory_space=pltpu.SMEM)
    return pl.pallas_call(
        top_kernel,
        in_specs=[s, s, v, v, v],
        out_specs=v,
        out_shape=jax.ShapeDtypeStruct((R, R), BF),
        compiler_params=pltpu.CompilerParams(vmem_limit_bytes=12 << 20),
        cost_estimate=pl.CostEstimate(flops=32 * 2 * R**3, bytes_accessed=3 << 20, transcendentals=0),
        name="top_far",
    )(info, src, own, other, mat)


def tail_kernel(info, src, c0, c1, c2, c3, c4a, c4b, c5, c6, c7, mat, down, top, base, both, out, table):
    i = pl.program_id(0)
    x, core, z, y = info[1], info[2], info[3], info[4]

    @pl.when(i == 0)
    def _():
        for s, ref in ((0, c0), (1, c1), (2, c2), (3, c3), (4, c4a), (4.5, c4b), (5, c5), (6, c6), (7, c7)):
            first = int(s * 32)

            def step(j, carry):
                v = ref[pl.ds(pl.multiple_of(j * R, R), R), :]
                table[first + 2 * j] = v[:, :R]
                table[first + 2 * j + 1] = v[:, R:]
                return carry

            lax.fori_loop(0, ref.shape[0] // R, step, 0, unroll=4)

    acc = dot(down[0], top[...])
    rows = []
    for n in range(16):
        g = jnp.clip(src[i, n] - info[5], 0, Z * Y * 8 - 1)
        sy = lax.rem(y - lax.rem(g // 8, Y) + Y, Y)
        sz = lax.rem(z - g // (8 * Y) + Z, Z)
        rows.append(table[(sz * Y + sy) * 8 + lax.rem(g, 8)])
    for q in range(4):
        acc += dot(wide([mat[0, 4 * q + n] for n in range(4)]), jnp.concatenate(rows[4 * q : 4 * q + 4], axis=0))
    local = acc.astype(BF)
    res = dot(both[...].reshape(8 * R, R), local).reshape(8, R, R)
    out[...] = (base[...] + res).astype(BF)


def tail(info, src, chunks, mat, down, top, base, both):
    def const(a):
        return pl.BlockSpec(a.shape, lambda i, *_: (0, 0))

    leaf = pl.BlockSpec((8, R, R), lambda i, *_: (i, 0, 0))
    return pl.pallas_call(
        tail_kernel,
        grid_spec=pltpu.PrefetchScalarGridSpec(
            num_scalar_prefetch=2,
            grid=(8,),
            in_specs=[const(c) for c in chunks]
            + [
                pl.BlockSpec((1, 16, R, R), lambda i, *_: (i, 0, 0, 0)),
                pl.BlockSpec((1, R, R), lambda i, *_: (i, 0, 0)),
                const(top),
                leaf,
                leaf,
            ],
            out_specs=leaf,
            scratch_shapes=[VMEM((256, R, R), BF)],
        ),
        out_shape=jax.ShapeDtypeStruct((64, R, R), BF),
        compiler_params=pltpu.CompilerParams(vmem_limit_bytes=24 << 20),
        cost_estimate=pl.CostEstimate(flops=200 * 2 * R**3, bytes_accessed=9 << 20, transcendentals=0),
        name="tail",
    )(info, src, *chunks, mat, down, top, base, both)


def place(d):
    return d // (CORE * Z * Y), d // (Z * Y) % CORE, d // Y % Z, d % Y


def index(x, c, z, y):
    return ((x % X * CORE + c % CORE) * Z + z % Z) * Y + y % Y


def shift(a, x=0, c=0, z=0, y=0):
    pairs = []
    for d in range(X * CORE * Z * Y):
        px, pc, pz, py = place(d)
        pairs.append((d, index(px + x, pc + c, pz + z, py + y)))
    return lax.ppermute(a, BOTH, pairs)


def halo(a):
    n = X * CORE * Z * Y
    up = [(i, i + 1) for i in range(n - 1)]
    return lax.ppermute(a, BOTH, up), lax.ppermute(a, BOTH, [(j, i) for i, j in up])


def shards(
    charges,
    source_basis,
    target_basis,
    leaf_up,
    mid_up,
    leaf_down,
    mid_down,
    leaf_far_src,
    leaf_far_mat,
    mid_far_src,
    mid_far_mat,
    top_far_src,
    top_far_mat,
    near_src,
    near_count,
    near_mat,
):
    me = lax.axis_index(BOTH).astype(jnp.int32)
    px, pc, pz, py = place(me)
    info = jnp.stack([(me - 1) * 64, px, pc, pz, py, me // (Z * Y) * (Z * Y * 8)])

    packed, coef, mt = upsweep(charges, source_basis, leaf_up, mid_up)

    by_y = [mt] + [shift(mt, y=s) for s in range(1, Y)]
    mids = jnp.concatenate([a[:256] for a in by_y], axis=0)
    tops = jnp.concatenate([a[256:] for a in by_y], axis=0)

    before, after = halo(packed)
    coef_before, coef_after = halo(coef)

    all_z = jnp.concatenate([tops] + [shift(tops, z=s) for s in range(1, Z)], axis=0)
    f1, b1 = shift(mids, z=1), shift(mids, z=-1)
    f2, b2 = shift(f1, z=1), shift(b1, z=-1)
    f3, b3 = shift(f2, z=1), shift(b2, z=-1)
    f4, b4 = shift(f3[:512], z=1), shift(b3[512:], z=-1)

    all_x = jnp.concatenate([all_z] + [shift(all_z, x=s) for s in range(1, X)], axis=0)
    other = shift(all_x, c=1)

    near = near_field(info, near_src.T, near_count, before, packed, after, near_mat)
    base, both = leaf_far(
        info, leaf_far_src.T, coef_before, coef, coef_after, leaf_far_mat, target_basis, leaf_down, near
    )
    top_local = top_far(info, top_far_src, all_x, other, top_far_mat)
    chunks = [mids, f1, f2, f3, f4, b4, b3, b2, b1]
    return tail(info, mid_far_src, chunks, mid_far_mat, mid_down, top_local, base, both)


def solution(mesh):
    row = P(BOTH, None)
    three = P(BOTH, None, None)
    four = P(BOTH, None, None, None)
    in_specs = (
        three, three, three, three, three, three, three,
        row, four, row, four, row, four, row, P(BOTH), four,
    )
    return jax.shard_map(shards, mesh=mesh, in_specs=in_specs, out_specs=three, check_vma=False)
```

time: 275 us -> 127 us (0.46)
  waiting for transfers between devices: 139 us -> 11.6 us
  local copies, waits for them, and re-layouts: 66.2 us -> 17.8 us
  Pallas kernels: 0 us -> 37.2 us
  starting transfers between devices: 22.2 us -> 59 us
  matrix products: 26.1 us -> 0 us
  between operations: 13.7 us -> 0.45 us
  other arithmetic: 7.41 us -> 0.02 us
    all_gather x2 -> x0, waiting for transfers between devices: 105 us -> none  [the longest x1 105 us: shards(): lax.all_gather(top_coef, ('cluster', 'coupling'), axis=0, tiled=True)]
    gather x5 -> x0, local copies, waits for them, and re-layouts: 62.7 us -> none  [the longest x2 33.5 us: shards(): picked = padded_charges[near_local] * near_used[:, :, None, None]]
    pallas_call x0 -> x5, Pallas kernels: none -> 37.2 us  [the longest x1 15.9 us: leaf_far(): pl.pallas_call(far_kernel, grid_spec=pltpu.PrefetchScalarGridSpec(num_sca...]
    ppermute x4 -> x26, starting transfers between devices: 22.1 us -> 59 us  [the longest x22 40.6 us: shift(): return lax.ppermute(a, BOTH, pairs)]
    dot_general x9 -> x0, matrix products: 26.1 us -> none  [product(): return jnp.einsum(form, left, right, preferred_element_type=jnp.float32)]
    ppermute x4 -> x26, waiting for transfers between devices: 34.1 us -> 11.6 us  [the longest x22 7.57 us: shift(): return lax.ppermute(a, BOTH, pairs)]
    unnamed x22 -> x72, local copies, waits for them, and re-layouts: 0.04 us -> 16.3 us
    concatenate x2, other arithmetic: 6.72 us -> 0.02 us  [the longest x1 0.02 us: shards(): mids = jnp.concatenate([a[:256] for a in by_y], axis=0)]
  transfers between devices with their start and end apart: 6 -> 26, of which waited for: 2 -> 5; matrix products, arithmetic and copies ran while one was open for 26% -> 1% of each run, Pallas kernels for 0% -> 20%
where the time goes in v1:
time: 127 us; the launch traced here: 126 us
  starting transfers between devices  59 us (46%)
  Pallas kernels  37.2 us (29%)
  local copies, waits for them, and re-layouts  17.8 us (14%)
  waiting for transfers between devices  11.6 us (9%)
    ppermute x22, starting transfers between devices, shift(): return lax.ppermute(a, BOTH, pairs)  40.6 us
    unnamed x72, local copies, waits for them, and re-layouts  16.3 us
    pallas_call x1, Pallas kernels, leaf_far(): pl.pallas_call(far_kernel, grid_spec=pltpu.PrefetchScalarGridSpec(num_sca...  15.9 us
    ppermute x2, starting transfers between devices, halo(): lax.ppermute(a, BOTH, [(j, i) for i, j in up])  14.5 us
    pallas_call x1, Pallas kernels, tail(): pl.pallas_call(tail_kernel, grid_spec=pltpu.PrefetchScalarGridSpec(num_sc...  10.2 us
    ppermute x22, waiting for transfers between devices, shift(): return lax.ppermute(a, BOTH, pairs)  7.57 us
    pallas_call x1, Pallas kernels, near_field(): pl.pallas_call(near_kernel, grid_spec=pltpu.PrefetchScalarGridSpec(num_sc...  7.31 us
    ppermute x2, waiting for transfers between devices, halo(): lax.ppermute(a, BOTH, up)  4.05 us
  transfers between devices with their start and end apart: 26, of which 5 were waited for; matrix products, arithmetic and copies ran while one was open for 1% of the time, Pallas kernels for 20%

profile of v1, /device:TPU:1, one launch (start us, length us, event | category | flops | bytes accessed | tf_op | source)
XLA Modules:
  0.0 126.1 jit_solution(1680917018002093920)
XLA Ops:
  4.6 2.2 %upsweep.1 = (bf16[32,64,128]{2,1,0:T(8,128)(2,1)S(1)}, bf16[32,64,128]{2,1,0:T(8,128)(2,1)S(1)}, bf16[288,128]{1,0:T(8,128)(2,1)S(1)}) custom-call(bf16[64,64,64]{2,1,0:T(8,128)(2,1)S(1)} %copy-done.3, bf16[64,64,64]{2,1,0:T(8,128)(2,1)S(1)} %copy-done.4, bf16[64,64,64]{2,1,0:T(8,128)(2,1)S(1)} %copy-done.5, bf16[8,64,64]{2,1,0:T(8,128)(2,1)S(1)} %copy-done.24), custom_call_target="tpu_custom_call" | custom-call | flops 71303168 | bytes 5242880 | tf_op jit(solution)/shard_map/upsweep/pallas_call | solution.py:63
  6.8 2.2 %collective-permute-start = (bf16[288,128]{1,0:T(8,128)(2,1)S(1)}, bf16[288,128]{1,0:T(8,128)(2,1)S(1)}, u32[]{:S(2)}, u32[]{:S(2)}) collective-permute-start(bf16[288,128]{1,0:T(8,128)(2,1)S(1)} %get-tuple-element.10), channel_id=1, source_target_pairs={{0,1},{1,2},{2,3},{3,0},{4,5},{5,6},{6,7},{7,4},{8,9},{9,10},{10,1... | collective-permute-start | bytes 221192 | tf_op jit(solution)/shard_map/ppermute | solution.py:267
  8.9 2.6 %collective-permute-start.1 = (bf16[288,128]{1,0:T(8,128)(2,1)S(1)}, bf16[288,128]{1,0:T(8,128)(2,1)S(1)}, u32[]{:S(2)}, u32[]{:S(2)}) collective-permute-start(bf16[288,128]{1,0:T(8,128)(2,1)S(1)} %get-tuple-element.10), channel_id=1, source_target_pairs={{0,2},{1,3},{2,0},{3,1},{4,6},{5,7},{6,4},{7,5},{8,10},{9,11},{10,... | collective-permute-start | bytes 221192 | tf_op jit(solution)/shard_map/ppermute | solution.py:267
  12.7 1.8 %collective-permute-done.1 = bf16[288,128]{1,0:T(8,128)(2,1)S(1)} collective-permute-done((bf16[288,128]{1,0:T(8,128)(2,1)S(1)}, bf16[288,128]{1,0:T(8,128)(2,1)S(1)}, u32[]{:S(2)}, u32[]{:S(2)}) %collective-permute-start.1) | collective-permute-done | bytes 73760 | tf_op jit(solution)/shard_map/ppermute | solution.py:267
  15.1 1.8 %collective-permute-start.11 = (bf16[128,128]{1,0:T(8,128)(2,1)S(1)}, bf16[128,128]{1,0:T(8,128)(2,1)S(1)}, u32[]{:S(2)}, u32[]{:S(2)}) collective-permute-start(bf16[128,128]{1,0:T(8,128)(2,1)S(1)} %pad_maximum_fusion.1), channel_id=1, source_target_pairs={{0,4},{1,5},{2,6},{3,7},{4,8},{5,9},{6,10},{7,11},{8,12},{9,13},{1... | collective-permute-start | bytes 98312 | tf_op jit(solution)/shard_map/ppermute | solution.py:267
  16.9 3.0 %collective-permute-start.12 = (bf16[128,128]{1,0:T(8,128)(2,1)S(1)}, bf16[128,128]{1,0:T(8,128)(2,1)S(1)}, u32[]{:S(2)}, u32[]{:S(2)}) collective-permute-start(bf16[128,128]{1,0:T(8,128)(2,1)S(1)} %pad_maximum_fusion.1), channel_id=1, source_target_pairs={{0,8},{1,9},{2,10},{3,11},{4,12},{5,13},{6,14},{7,15},{8,16},{9,17... | collective-permute-start | bytes 98312 | tf_op jit(solution)/shard_map/ppermute | solution.py:267
  19.9 3.8 %collective-permute-start.13 = (bf16[128,128]{1,0:T(8,128)(2,1)S(1)}, bf16[128,128]{1,0:T(8,128)(2,1)S(1)}, u32[]{:S(2)}, u32[]{:S(2)}) collective-permute-start(bf16[128,128]{1,0:T(8,128)(2,1)S(1)} %pad_maximum_fusion.1), channel_id=1, source_target_pairs={{0,12},{1,13},{2,14},{3,15},{4,16},{5,17},{6,18},{7,19},{8,20},{9,... | collective-permute-start | bytes 98312 | tf_op jit(solution)/shard_map/ppermute | solution.py:267
  24.1 4.5 %collective-permute-start.15 = (bf16[128,128]{1,0:T(8,128)(2,1)S(1)}, bf16[128,128]{1,0:T(8,128)(2,1)S(1)}, u32[]{:S(2)}, u32[]{:S(2)}) collective-permute-start(bf16[128,128]{1,0:T(8,128)(2,1)S(1)} %pad_maximum_fusion.1), channel_id=1, source_target_pairs={{0,20},{1,21},{2,22},{3,23},{4,24},{5,25},{6,26},{7,27},{8,28},{9,... | collective-permute-start | bytes 98312 | tf_op jit(solution)/shard_map/ppermute | solution.py:267
  28.6 2.5 %collective-permute-start.16 = (bf16[128,128]{1,0:T(8,128)(2,1)S(1)}, bf16[128,128]{1,0:T(8,128)(2,1)S(1)}, u32[]{:S(2)}, u32[]{:S(2)}) collective-permute-start(bf16[128,128]{1,0:T(8,128)(2,1)S(1)} %pad_maximum_fusion.1), channel_id=1, source_target_pairs={{0,24},{1,25},{2,26},{3,27},{4,28},{5,29},{6,30},{7,31},{8,0},{9,1... | collective-permute-start | bytes 98312 | tf_op jit(solution)/shard_map/ppermute | solution.py:267
  36.1 2.5 %collective-permute-start.19 = (bf16[1024,128]{1,0:T(8,128)(2,1)S(1)}, bf16[1024,128]{1,0:T(8,128)(2,1)S(1)}, u32[]{:S(2)}, u32[]{:S(2)}) collective-permute-start(bf16[1024,128]{1,0:T(8,128)(2,1)S(1)} %get-tuple-element.27), channel_id=1, source_target_pairs={{0,128},{1,129},{2,130},{3,131},{4,132},{5,133},{6,134},{7,135},{8... | collective-permute-start | bytes 786440 | tf_op jit(solution)/shard_map/ppermute | solution.py:267
  39.7 2.1 %collective-permute-start.8 = (bf16[1024,128]{1,0:T(8,128)(2,1)S(1)}, bf16[1024,128]{1,0:T(8,128)(2,1)S(1)}, u32[]{:S(2)}, u32[]{:S(2)}) collective-permute-start(bf16[1024,128]{1,0:T(8,128)(2,1)S(1)} %collective-permute-done.7.c7), channel_id=1, source_target_pairs={{0,28},{1,29},{2,30},{3,31},{4,0},{5,1},{6,2},{7,3},{8,4},{9,5},{1... | collective-permute-start | bytes 786440 | tf_op jit(solution)/shard_map/ppermute | solution.py:267
  41.9 4.0 %collective-permute-done.19 = bf16[1024,128]{1,0:T(8,128)(2,1)S(1)} collective-permute-done((bf16[1024,128]{1,0:T(8,128)(2,1)S(1)}, bf16[1024,128]{1,0:T(8,128)(2,1)S(1)}, u32[]{:S(2)}, u32[]{:S(2)}) %collective-permute-start.19) | collective-permute-done | bytes 262176 | tf_op jit(solution)/shard_map/ppermute | solution.py:267
  46.0 5.6 %collective-permute-start.21 = (bf16[4096,128]{1,0:T(8,128)(2,1)S(1)}, bf16[4096,128]{1,0:T(8,128)(2,1)S(1)}, u32[]{:S(2)}, u32[]{:S(2)}) collective-permute-start(bf16[4096,128]{1,0:T(8,128)(2,1)S(1)} %constant_dynamic-update-slice_fusion.11.own), channel_id=1, source_target_pairs={{0,32},{1,33},{2,34},{3,35},{4,36},{5,37},{6,38},{7,39},{8,40},{9,... | collective-permute-start | bytes 3145736 | tf_op jit(solution)/shard_map/ppermute | solution.py:267
  51.6 2.2 %collective-permute-start.9 = (bf16[1024,128]{1,0:T(8,128)(2,1)S(1)}, bf16[1024,128]{1,0:T(8,128)(2,1)S(1)}, u32[]{:S(2)}, u32[]{:S(2)}) collective-permute-start(bf16[1024,128]{1,0:T(8,128)(2,1)S(1)} %collective-permute-done.8.c6), channel_id=1, source_target_pairs={{0,28},{1,29},{2,30},{3,31},{4,0},{5,1},{6,2},{7,3},{8,4},{9,5},{1... | collective-permute-start | bytes 786440 | tf_op jit(solution)/shard_map/ppermute | solution.py:267
  53.9 2.1 %collective-permute-start.24 = (bf16[32,64,128]{2,1,0:T(8,128)(2,1)S(1)}, bf16[32,64,128]{2,1,0:T(8,128)(2,1)S(1)}, u32[]{:S(2)}, u32[]{:S(2)}) collective-permute-start(bf16[32,64,128]{2,1,0:T(8,128)(2,1)S(1)} %get-tuple-element.12.own), channel_id=1, source_target_pairs={{0,1},{1,2},{2,3},{3,4},{4,5},{5,6},{6,7},{7,8},{8,9},{9,10},{10,1... | collective-permute-start | bytes 1572872 | tf_op jit(solution)/shard_map/ppermute | solution.py:273
  56.0 7.5 %collective-permute-start.25 = (bf16[32,64,128]{2,1,0:T(8,128)(2,1)S(1)}, bf16[32,64,128]{2,1,0:T(8,128)(2,1)S(1)}, u32[]{:S(2)}, u32[]{:S(2)}) collective-permute-start(bf16[32,64,128]{2,1,0:T(8,128)(2,1)S(1)} %get-tuple-element.12.own), channel_id=1, source_target_pairs={{1,0},{2,1},{3,2},{4,3},{5,4},{6,5},{7,6},{8,7},{9,8},{10,9},{11,1... | collective-permute-start | bytes 1572872 | tf_op jit(solution)/shard_map/ppermute | solution.py:273
  63.5 1.9 %collective-permute-start.22 = (bf16[32,64,128]{2,1,0:T(8,128)(2,1)S(1)}, bf16[32,64,128]{2,1,0:T(8,128)(2,1)}, u32[]{:S(2)}, u32[]{:S(2)}) collective-permute-start(bf16[32,64,128]{2,1,0:T(8,128)(2,1)S(1)} %get-tuple-element.11.own), channel_id=1, source_target_pairs={{0,1},{1,2},{2,3},{3,4},{4,5},{5,6},{6,7},{7,8},{8,9},{9,10},{10,1... | collective-permute-start | bytes 1572872 | tf_op jit(solution)/shard_map/ppermute | solution.py:273
  65.5 7.0 %collective-permute-start.23 = (bf16[32,64,128]{2,1,0:T(8,128)(2,1)S(1)}, bf16[32,64,128]{2,1,0:T(8,128)(2,1)}, u32[]{:S(2)}, u32[]{:S(2)}) collective-permute-start(bf16[32,64,128]{2,1,0:T(8,128)(2,1)S(1)} %get-tuple-element.11.own), channel_id=1, source_target_pairs={{1,0},{2,1},{3,2},{4,3},{5,4},{6,5},{7,6},{8,7},{9,8},{10,9},{11,1... | collective-permute-start | bytes 1572872 | tf_op jit(solution)/shard_map/ppermute | solution.py:273
  73.8 4.1 %collective-permute-done.24.bef = bf16[32,64,128]{2,1,0:T(8,128)(2,1)S(1)} collective-permute-done((bf16[32,64,128]{2,1,0:T(8,128)(2,1)S(1)}, bf16[32,64,128]{2,1,0:T(8,128)(2,1)S(1)}, u32[]{:S(2)}, u32[]{:S(2)}) %collective-permute-start.24) | collective-permute-done | bytes 524320 | tf_op jit(solution)/shard_map/ppermute | solution.py:273
  81.0 3.4 %copy-done.1 = bf16[64,8,64,64]{3,2,1,0:T(8,128)(2,1)S(1)} copy-done((bf16[64,8,64,64]{3,2,1,0:T(8,128)(2,1)S(1)}, bf16[64,8,64,64]{3,2,1,0:T(8,128)(2,1)}, u32[]{:S(2)}) %copy-start.1) | copy-done | bytes 4194328
  87.5 7.3 %near.1 = f32[64,64,64]{2,1,0:T(8,128)S(1)} custom-call(s32[6]{0:T(128)S(1)} %stack.27.info, s32[8,64]{1,0:T(8,128)S(1)} %bitcast.8, s32[64]{0:T(128)S(1)} %copy-done.28, bf16[32,64,128]{2,1,0:T(8,128)(2,1)S(1)} %copy-done.12, bf16[32,64,128]{2,1,0:T(8,128)(2,1)S(1)} %copy-done.10, bf16[32,64,128]{2,1,0:T(8,128)(2,1)S(1)} %copy-done.14, ...), custom_call_target="tpu_custom_call" | custom-call | flops 268435456 | bytes 12582912 | tf_op jit(solution)/shard_map/near/pallas_call | solution.py:111
  94.9 3.4 %copy-done = bf16[64,8,64,64]{3,2,1,0:T(8,128)(2,1)S(1)} copy-done((bf16[64,8,64,64]{3,2,1,0:T(8,128)(2,1)S(1)}, bf16[64,8,64,64]{3,2,1,0:T(8,128)(2,1)}, u32[]{:S(2)}) %copy-start) | copy-done | bytes 4194328
  98.3 15.9 %leaf_far.1 = (f32[64,64,64]{2,1,0:T(8,128)S(1)}, bf16[64,64,64]{2,1,0:T(8,128)(2,1)S(1)}) custom-call(s32[6]{0:T(128)S(1)} %stack.27.info, s32[8,64]{1,0:T(8,128)S(1)} %bitcast.9, bf16[32,64,128]{2,1,0:T(8,128)(2,1)} %collective-permute-done.22.bef, bf16[32,64,128]{2,1,0:T(8,128)(2,1)S(1)} %get-tuple-element.11.own, ...), custom_call_target="tpu_custom_call" | custom-call | flops 335544320 | bytes 16777216 | tf_op jit(solution)/shard_map/leaf_far/pallas_call | solution.py:147
  115.9 10.2 %tail.1 = bf16[64,64,64]{2,1,0:T(8,128)(2,1)} custom-call(s32[6]{0:T(128)S(1)} %stack.27.info, s32[8,16]{1,0:T(8,128)S(1)} %copy-done.27, bf16[1024,128]{1,0:T(8,128)(2,1)S(1)} %pad_maximum_fusion.c0, bf16[1024,128]{1,0:T(8,128)(2,1)S(1)} %copy-done.18, bf16[1024,128]{1,0:T(8,128)(2,1)S(1)} %copy-done.22, bf16[1024,128]{1,0:T(8,128)(2,1)S(1)} %collective-permute-done.5.c3, ...), custom_call_target="tpu_custom_call" | custom-call | flops 104857600 | bytes 9437184 | tf_op jit(solution)/shard_map/tail/pallas_call | solution.py:231
  (116 shorter events, 22.3 us)
Async XLA Ops:
  6.8 5.9 %collective-permute-start = (bf16[288,128]{1,0:T(8,128)(2,1)S(1)}, bf16[288,128]{1,0:T(8,128)(2,1)S(1)}, u32[]{:S(2)}, u32[]{:S(2)}) collective-permute-start(bf16[288,128]{1,0:T(8,128)(2,1)S(1)} %get-tuple-element.10), channel_id=1, source_target_pairs={{0,1},{1,2},{2,3},{3,0},{4,5},{5,6},{6,7},{7,4},{8,9},{9,10},{10,1... | collective-permute-start | bytes 221192 | tf_op jit(solution)/shard_map/ppermute | solution.py:267
  8.9 5.6 %collective-permute-start.1 = (bf16[288,128]{1,0:T(8,128)(2,1)S(1)}, bf16[288,128]{1,0:T(8,128)(2,1)S(1)}, u32[]{:S(2)}, u32[]{:S(2)}) collective-permute-start(bf16[288,128]{1,0:T(8,128)(2,1)S(1)} %get-tuple-element.10), channel_id=1, source_target_pairs={{0,2},{1,3},{2,0},{3,1},{4,6},{5,7},{6,4},{7,5},{8,10},{9,11},{10,... | collective-permute-start | bytes 221192 | tf_op jit(solution)/shard_map/ppermute | solution.py:267
  15.1 13.5 %collective-permute-start.11 = (bf16[128,128]{1,0:T(8,128)(2,1)S(1)}, bf16[128,128]{1,0:T(8,128)(2,1)S(1)}, u32[]{:S(2)}, u32[]{:S(2)}) collective-permute-start(bf16[128,128]{1,0:T(8,128)(2,1)S(1)} %pad_maximum_fusion.1), channel_id=1, source_target_pairs={{0,4},{1,5},{2,6},{3,7},{4,8},{5,9},{6,10},{7,11},{8,12},{9,13},{1... | collective-permute-start | bytes 98312 | tf_op jit(solution)/shard_map/ppermute | solution.py:267
  16.9 14.2 %collective-permute-start.12 = (bf16[128,128]{1,0:T(8,128)(2,1)S(1)}, bf16[128,128]{1,0:T(8,128)(2,1)S(1)}, u32[]{:S(2)}, u32[]{:S(2)}) collective-permute-start(bf16[128,128]{1,0:T(8,128)(2,1)S(1)} %pad_maximum_fusion.1), channel_id=1, source_target_pairs={{0,8},{1,9},{2,10},{3,11},{4,12},{5,13},{6,14},{7,15},{8,16},{9,17... | collective-permute-start | bytes 98312 | tf_op jit(solution)/shard_map/ppermute | solution.py:267
  19.9 12.1 %collective-permute-start.13 = (bf16[128,128]{1,0:T(8,128)(2,1)S(1)}, bf16[128,128]{1,0:T(8,128)(2,1)S(1)}, u32[]{:S(2)}, u32[]{:S(2)}) collective-permute-start(bf16[128,128]{1,0:T(8,128)(2,1)S(1)} %pad_maximum_fusion.1), channel_id=1, source_target_pairs={{0,12},{1,13},{2,14},{3,15},{4,16},{5,17},{6,18},{7,19},{8,20},{9,... | collective-permute-start | bytes 98312 | tf_op jit(solution)/shard_map/ppermute | solution.py:267
  23.6 8.4 %collective-permute-start.14 = (bf16[128,128]{1,0:T(8,128)(2,1)S(1)}, bf16[128,128]{1,0:T(8,128)(2,1)S(1)}, u32[]{:S(2)}, u32[]{:S(2)}) collective-permute-start(bf16[128,128]{1,0:T(8,128)(2,1)S(1)} %pad_maximum_fusion.1), channel_id=1, source_target_pairs={{0,16},{1,17},{2,18},{3,19},{4,20},{5,21},{6,22},{7,23},{8,24},{9,... | collective-permute-start | bytes 98312 | tf_op jit(solution)/shard_map/ppermute | solution.py:267
  24.1 9.5 %collective-permute-start.15 = (bf16[128,128]{1,0:T(8,128)(2,1)S(1)}, bf16[128,128]{1,0:T(8,128)(2,1)S(1)}, u32[]{:S(2)}, u32[]{:S(2)}) collective-permute-start(bf16[128,128]{1,0:T(8,128)(2,1)S(1)} %pad_maximum_fusion.1), channel_id=1, source_target_pairs={{0,20},{1,21},{2,22},{3,23},{4,24},{5,25},{6,26},{7,27},{8,28},{9,... | collective-permute-start | bytes 98312 | tf_op jit(solution)/shard_map/ppermute | solution.py:267
  28.6 5.0 %collective-permute-start.16 = (bf16[128,128]{1,0:T(8,128)(2,1)S(1)}, bf16[128,128]{1,0:T(8,128)(2,1)S(1)}, u32[]{:S(2)}, u32[]{:S(2)}) collective-permute-start(bf16[128,128]{1,0:T(8,128)(2,1)S(1)} %pad_maximum_fusion.1), channel_id=1, source_target_pairs={{0,24},{1,25},{2,26},{3,27},{4,28},{5,29},{6,30},{7,31},{8,0},{9,1... | collective-permute-start | bytes 98312 | tf_op jit(solution)/shard_map/ppermute | solution.py:267
  31.9 7.8 %collective-permute-start.7 = (bf16[1024,128]{1,0:T(8,128)(2,1)S(1)}, bf16[1024,128]{1,0:T(8,128)(2,1)S(1)}, u32[]{:S(2)}, u32[]{:S(2)}) collective-permute-start(bf16[1024,128]{1,0:T(8,128)(2,1)S(1)} %pad_maximum_fusion.c0), channel_id=1, source_target_pairs={{0,28},{1,29},{2,30},{3,31},{4,0},{5,1},{6,2},{7,3},{8,4},{9,5},{1... | collective-permute-start | bytes 786440 | tf_op jit(solution)/shard_map/ppermute | solution.py:267
  32.0 9.8 %collective-permute-start.3 = (bf16[1024,128]{1,0:T(8,128)(2,1)S(1)}, bf16[1024,128]{1,0:T(8,128)(2,1)S(1)}, u32[]{:S(2)}, u32[]{:S(2)}) collective-permute-start(bf16[1024,128]{1,0:T(8,128)(2,1)S(1)} %pad_maximum_fusion.c0), channel_id=1, source_target_pairs={{0,4},{1,5},{2,6},{3,7},{4,8},{5,9},{6,10},{7,11},{8,12},{9,13},{1... | collective-permute-start | bytes 786440 | tf_op jit(solution)/shard_map/ppermute | solution.py:267
  34.8 7.0 %collective-permute-start.18 = (bf16[1024,128]{1,0:T(8,128)(2,1)S(1)}, bf16[1024,128]{1,0:T(8,128)(2,1)S(1)}, u32[]{:S(2)}, u32[]{:S(2)}) collective-permute-start(bf16[1024,128]{1,0:T(8,128)(2,1)S(1)} %get-tuple-element.27), channel_id=1, source_target_pairs={{0,64},{1,65},{2,66},{3,67},{4,68},{5,69},{6,70},{7,71},{8,72},{9,... | collective-permute-start | bytes 786440 | tf_op jit(solution)/shard_map/ppermute | solution.py:267
  36.1 9.8 %collective-permute-start.19 = (bf16[1024,128]{1,0:T(8,128)(2,1)S(1)}, bf16[1024,128]{1,0:T(8,128)(2,1)S(1)}, u32[]{:S(2)}, u32[]{:S(2)}) collective-permute-start(bf16[1024,128]{1,0:T(8,128)(2,1)S(1)} %get-tuple-element.27), channel_id=1, source_target_pairs={{0,128},{1,129},{2,130},{3,131},{4,132},{5,133},{6,134},{7,135},{8... | collective-permute-start | bytes 786440 | tf_op jit(solution)/shard_map/ppermute | solution.py:267
  38.5 7.4 %collective-permute-start.20 = (bf16[1024,128]{1,0:T(8,128)(2,1)S(1)}, bf16[1024,128]{1,0:T(8,128)(2,1)S(1)}, u32[]{:S(2)}, u32[]{:S(2)}) collective-permute-start(bf16[1024,128]{1,0:T(8,128)(2,1)S(1)} %get-tuple-element.27), channel_id=1, source_target_pairs={{0,192},{1,193},{2,194},{3,195},{4,196},{5,197},{6,198},{7,199},{8... | collective-permute-start | bytes 786440 | tf_op jit(solution)/shard_map/ppermute | solution.py:267
  39.7 11.9 %collective-permute-start.8 = (bf16[1024,128]{1,0:T(8,128)(2,1)S(1)}, bf16[1024,128]{1,0:T(8,128)(2,1)S(1)}, u32[]{:S(2)}, u32[]{:S(2)}) collective-permute-start(bf16[1024,128]{1,0:T(8,128)(2,1)S(1)} %collective-permute-done.7.c7), channel_id=1, source_target_pairs={{0,28},{1,29},{2,30},{3,31},{4,0},{5,1},{6,2},{7,3},{8,4},{9,5},{1... | collective-permute-start | bytes 786440 | tf_op jit(solution)/shard_map/ppermute | solution.py:267
  41.8 12.0 %collective-permute-start.4 = (bf16[1024,128]{1,0:T(8,128)(2,1)S(1)}, bf16[1024,128]{1,0:T(8,128)(2,1)S(1)}, u32[]{:S(2)}, u32[]{:S(2)}) collective-permute-start(bf16[1024,128]{1,0:T(8,128)(2,1)S(1)} %collective-permute-done.3.c1), channel_id=1, source_target_pairs={{0,4},{1,5},{2,6},{3,7},{4,8},{5,9},{6,10},{7,11},{8,12},{9,13},{1... | collective-permute-start | bytes 786440 | tf_op jit(solution)/shard_map/ppermute | solution.py:267
  46.0 68.3 %collective-permute-start.21 = (bf16[4096,128]{1,0:T(8,128)(2,1)S(1)}, bf16[4096,128]{1,0:T(8,128)(2,1)S(1)}, u32[]{:S(2)}, u32[]{:S(2)}) collective-permute-start(bf16[4096,128]{1,0:T(8,128)(2,1)S(1)} %constant_dynamic-update-slice_fusion.11.own), channel_id=1, source_target_pairs={{0,32},{1,33},{2,34},{3,35},{4,36},{5,37},{6,38},{7,39},{8,40},{9,... | collective-permute-start | bytes 3145736 | tf_op jit(solution)/shard_map/ppermute | solution.py:267
  51.6 11.9 %collective-permute-start.9 = (bf16[1024,128]{1,0:T(8,128)(2,1)S(1)}, bf16[1024,128]{1,0:T(8,128)(2,1)S(1)}, u32[]{:S(2)}, u32[]{:S(2)}) collective-permute-start(bf16[1024,128]{1,0:T(8,128)(2,1)S(1)} %collective-permute-done.8.c6), channel_id=1, source_target_pairs={{0,28},{1,29},{2,30},{3,31},{4,0},{5,1},{6,2},{7,3},{8,4},{9,5},{1... | collective-permute-start | bytes 786440 | tf_op jit(solution)/shard_map/ppermute | solution.py:267
  53.8 11.6 %collective-permute-start.5 = (bf16[1024,128]{1,0:T(8,128)(2,1)S(1)}, bf16[1024,128]{1,0:T(8,128)(2,1)S(1)}, u32[]{:S(2)}, u32[]{:S(2)}) collective-permute-start(bf16[1024,128]{1,0:T(8,128)(2,1)S(1)} %collective-permute-done.4.c2), channel_id=1, source_target_pairs={{0,4},{1,5},{2,6},{3,7},{4,8},{5,9},{6,10},{7,11},{8,12},{9,13},{1... | collective-permute-start | bytes 786440 | tf_op jit(solution)/shard_map/ppermute | solution.py:267
  53.9 23.9 %collective-permute-start.24 = (bf16[32,64,128]{2,1,0:T(8,128)(2,1)S(1)}, bf16[32,64,128]{2,1,0:T(8,128)(2,1)S(1)}, u32[]{:S(2)}, u32[]{:S(2)}) collective-permute-start(bf16[32,64,128]{2,1,0:T(8,128)(2,1)S(1)} %get-tuple-element.12.own), channel_id=1, source_target_pairs={{0,1},{1,2},{2,3},{3,4},{4,5},{5,6},{6,7},{7,8},{8,9},{9,10},{10,1... | collective-permute-start | bytes 1572872 | tf_op jit(solution)/shard_map/ppermute | solution.py:273
  56.0 22.6 %collective-permute-start.25 = (bf16[32,64,128]{2,1,0:T(8,128)(2,1)S(1)}, bf16[32,64,128]{2,1,0:T(8,128)(2,1)S(1)}, u32[]{:S(2)}, u32[]{:S(2)}) collective-permute-start(bf16[32,64,128]{2,1,0:T(8,128)(2,1)S(1)} %get-tuple-element.12.own), channel_id=1, source_target_pairs={{1,0},{2,1},{3,2},{4,3},{5,4},{6,5},{7,6},{8,7},{9,8},{10,9},{11,1... | collective-permute-start | bytes 1572872 | tf_op jit(solution)/shard_map/ppermute | solution.py:273
  63.5 31.3 %collective-permute-start.22 = (bf16[32,64,128]{2,1,0:T(8,128)(2,1)S(1)}, bf16[32,64,128]{2,1,0:T(8,128)(2,1)}, u32[]{:S(2)}, u32[]{:S(2)}) collective-permute-start(bf16[32,64,128]{2,1,0:T(8,128)(2,1)S(1)} %get-tuple-element.11.own), channel_id=1, source_target_pairs={{0,1},{1,2},{2,3},{3,4},{4,5},{5,6},{6,7},{7,8},{8,9},{9,10},{10,1... | collective-permute-start | bytes 1572872 | tf_op jit(solution)/shard_map/ppermute | solution.py:273
  65.5 29.4 %collective-permute-start.23 = (bf16[32,64,128]{2,1,0:T(8,128)(2,1)S(1)}, bf16[32,64,128]{2,1,0:T(8,128)(2,1)}, u32[]{:S(2)}, u32[]{:S(2)}) collective-permute-start(bf16[32,64,128]{2,1,0:T(8,128)(2,1)S(1)} %get-tuple-element.11.own), channel_id=1, source_target_pairs={{1,0},{2,1},{3,2},{4,3},{5,4},{6,5},{7,6},{8,7},{9,8},{10,9},{11,1... | collective-permute-start | bytes 1572872 | tf_op jit(solution)/shard_map/ppermute | solution.py:273
  78.6 37.2 %collective-permute-start.10 = (bf16[512,128]{1,0:T(8,128)(2,1)}, bf16[512,128]{1,0:T(8,128)(2,1)S(1)}, u32[]{:S(2)}, u32[]{:S(2)}) collective-permute-start(bf16[512,128]{1,0:T(8,128)(2,1)} %slice.44), channel_id=1, source_target_pairs={{0,28},{1,29},{2,30},{3,31},{4,0},{5,1},{6,2},{7,3},{8,4},{9,5},{1... | collective-permute-start | bytes 393224 | tf_op jit(solution)/shard_map/ppermute | solution.py:267
  79.4 36.4 %collective-permute-start.6 = (bf16[512,128]{1,0:T(8,128)(2,1)}, bf16[512,128]{1,0:T(8,128)(2,1)}, u32[]{:S(2)}, u32[]{:S(2)}) collective-permute-start(bf16[512,128]{1,0:T(8,128)(2,1)} %slice.43), channel_id=1, source_target_pairs={{0,4},{1,5},{2,6},{3,7},{4,8},{5,9},{6,10},{7,11},{8,12},{9,13},{1... | collective-permute-start | bytes 393224 | tf_op jit(solution)/shard_map/ppermute | solution.py:267
  (32 other events, 410.2 us)

commit v2 on v1

v2 whole, which is shorter than its diff:
```python
import jax
import jax.numpy as jnp
from jax import lax
from jax.experimental import pallas as pl
from jax.experimental.pallas import tpu as pltpu
from jax.sharding import PartitionSpec as P

BOTH = ("cluster", "coupling")
X, CORE, Z, Y = 4, 2, 8, 4
R = 64
BF = jnp.bfloat16
F32 = jnp.float32
VMEM = pltpu.VMEM
BIG = 46 << 20
SMALL = 8 << 20


def dot(a, b):
    return lax.dot_general(a, b, (((1,), (0,)), ((), ())), preferred_element_type=F32)


def dot_t(a, b):
    return lax.dot_general(a, b, (((0,), (0,)), ((), ())), preferred_element_type=F32)


def beside(a, b):
    return jnp.concatenate([a, b], axis=1)


def wide(blocks):
    return jnp.concatenate([beside(a, b) for a, b in zip(blocks[::2], blocks[1::2])], axis=1)


def up_kernel(c_ref, s_ref, lu_ref, mu_ref, pc_ref, pk_ref, mt_ref, acc):
    i = pl.program_id(0)

    @pl.when(i == 0)
    def _():
        acc[...] = jnp.zeros_like(acc)

    coefs = []
    for l in range(16):
        coefs.append(dot_t(s_ref[l], c_ref[l]).astype(BF))
    for j in range(8):
        pc_ref[j] = beside(c_ref[2 * j], c_ref[2 * j + 1])
        pk_ref[j] = beside(coefs[2 * j], coefs[2 * j + 1])
    mids = []
    for h in range(2):
        up = lu_ref[8 * h : 8 * h + 8].reshape(8 * R, R)
        mids.append(dot_t(up, jnp.concatenate(coefs[8 * h : 8 * h + 8], axis=0)).astype(BF))
    mt_ref[pl.ds(pl.multiple_of(i * R, R), R), :] = beside(*mids)
    acc[...] += dot_t(mu_ref[...].reshape(2 * R, R), jnp.concatenate(mids, axis=0))

    @pl.when(i == 3)
    def _():
        top = acc[...].astype(BF)
        mt_ref[256:288, :] = beside(top[:32], top[32:])


def upsweep(charges, source_basis, leaf_up, mid_up):
    leaf = pl.BlockSpec((16, R, R), lambda i: (i, 0, 0))
    pair = pl.BlockSpec((8, R, 2 * R), lambda i: (i, 0, 0))
    return pl.pallas_call(
        up_kernel,
        grid=(4,),
        in_specs=[leaf, leaf, leaf, pl.BlockSpec((2, R, R), lambda i: (i, 0, 0))],
        out_specs=[pair, pair, pl.BlockSpec((288, 128), lambda i: (0, 0))],
        out_shape=[
            jax.ShapeDtypeStruct((32, R, 2 * R), BF),
            jax.ShapeDtypeStruct((32, R, 2 * R), BF),
            jax.ShapeDtypeStruct((288, 128), BF),
        ],
        scratch_shapes=[VMEM((R, R), F32)],
        compiler_params=pltpu.CompilerParams(vmem_limit_bytes=60 << 20),
        cost_estimate=pl.CostEstimate(flops=136 * 2 * R**3, bytes_accessed=5 << 20, transcendentals=0),
        name="upsweep",
    )(charges, source_basis, leaf_up, mid_up)


def copies_of(pairs, sems):
    out = [pltpu.make_async_copy(a, b, sems.at[k]) for k, (a, b) in enumerate(pairs)]
    for c in out:
        c.start()
    return out


def parts(a, b, n):
    w = a.shape[0] // n
    return [(a.at[pl.ds(k * w, w)], b.at[pl.ds(k * w, w)]) for k in range(n)]


def half_masks(mask):
    lane = lax.broadcasted_iota(jnp.int32, (R, 2 * R), 1)
    mask[0] = jnp.where(lane < R, 1.0, 0.0).astype(BF)
    mask[1] = jnp.where(lane < R, 0.0, 1.0).astype(BF)
    mask[2] = jnp.zeros((R, 2 * R), BF)


def fold(acc):
    return acc[:, :R] + acc[:, R:]


def near_kernel(
    info, src, cnt, cb, co, ca, mat, fmat, tb, ld, out, fm, tbv, both, table, mv, ldv, mask, sem
):
    tables = copies_of([(cb, table.at[0:32]), (co, table.at[32:64]), (ca, table.at[64:96])], sem)
    copies_of(parts(mat, mv, 8), sem.at[pl.ds(3, 8)])
    small = copies_of([(tb, tbv), (ld, ldv)], sem.at[pl.ds(11, 2)])
    late = copies_of(parts(fmat, fm, 8), sem.at[pl.ds(13, 8)])
    half_masks(mask)
    for c in tables:
        c.wait()

    def step(c, carry):
        pltpu.make_async_copy(mat.at[pl.ds(8 * c, 8)], mv.at[pl.ds(8 * c, 8)], sem.at[3 + c]).wait()
        for g in range(2):
            accs = []
            for j in range(4):
                l = c * 8 + g * 4 + j
                acc = jnp.zeros((R, 2 * R), F32)
                for n in range(8):
                    k = jnp.clip(src[n, l] - info[0], 0, 191)
                    m = mask[jnp.where(n < cnt[l], k & 1, 2)]
                    acc += dot(mv[l, n], table[k >> 1] * m)
                accs.append(acc)
            for j in range(4):
                out[c * 8 + g * 4 + j] = fold(accs[j])
        return carry

    lax.fori_loop(0, 8, step, 0)
    for c in small:
        c.wait()

    def products(i, carry):
        res = [dot(tbv[8 * i + j], ldv[8 * i + j]).astype(BF) for j in range(8)]
        for j in range(8):
            both[8 * i + j] = res[j]
        return carry

    lax.fori_loop(0, 8, products, 0)
    for c in late:
        c.wait()


def near_field(info, src, cnt, charges, mat, fmat, tb, ld):
    v = pl.BlockSpec(memory_space=VMEM)
    s = pl.BlockSpec(memory_space=pltpu.SMEM)
    mats, leaf = VMEM((64, 8, R, R), BF), VMEM((64, R, R), BF)
    return pl.pallas_call(
        near_kernel,
        in_specs=[s] * 3 + [pl.BlockSpec(memory_space=pl.ANY)] * 7,
        out_specs=[v] * 4,
        out_shape=[VMEM((64, R, R), F32), mats, leaf, leaf],
        scratch_shapes=[
            VMEM((96, R, 2 * R), BF),
            mats,
            leaf,
            VMEM((3, R, 2 * R), BF),
            pltpu.SemaphoreType.DMA((21,)),
        ],
        compiler_params=pltpu.CompilerParams(vmem_limit_bytes=BIG),
        cost_estimate=pl.CostEstimate(flops=576 * 2 * R**3, bytes_accessed=24 << 20, transcendentals=0),
        name="near",
    )(info, src, cnt, *charges, mat, fmat, tb, ld)


def far_kernel(info, src, ku, ko, kd, mv, tbv, near, base, table, far, mask, sem):
    tables = copies_of([(ku, table.at[0:32]), (ko, table.at[32:64]), (kd, table.at[64:96])], sem)
    half_masks(mask)
    for c in tables:
        c.wait()

    def leaf(c, carry):
        for g in range(2):
            accs = []
            for j in range(4):
                l = c * 8 + g * 4 + j
                acc = jnp.zeros((R, 2 * R), F32)
                for n in range(8):
                    k = jnp.clip(src[n, l] - info[0], 0, 191)
                    acc += dot(mv[l, n], table[k >> 1] * mask[k & 1])
                accs.append(acc)
            for j in range(4):
                far[c * 8 + g * 4 + j] = fold(accs[j]).astype(BF)
        return carry

    lax.fori_loop(0, 8, leaf, 0)

    def last(i, carry):
        res = [near[8 * i + j] + dot(tbv[8 * i + j], far[8 * i + j]) for j in range(8)]
        for j in range(8):
            base[8 * i + j] = res[j]
        return carry

    lax.fori_loop(0, 8, last, 0)


def leaf_far(info, src, coefs, mat, tb, near):
    v = pl.BlockSpec(memory_space=VMEM)
    s = pl.BlockSpec(memory_space=pltpu.SMEM)
    return pl.pallas_call(
        far_kernel,
        in_specs=[s] * 2 + [pl.BlockSpec(memory_space=pl.ANY)] * 3 + [v] * 3,
        out_specs=v,
        out_shape=VMEM((64, R, R), F32),
        scratch_shapes=[
            VMEM((96, R, 2 * R), BF),
            VMEM((64, R, R), BF),
            VMEM((3, R, 2 * R), BF),
            pltpu.SemaphoreType.DMA((3,)),
        ],
        compiler_params=pltpu.CompilerParams(vmem_limit_bytes=32 << 20),
        cost_estimate=pl.CostEstimate(flops=576 * 2 * R**3, bytes_accessed=16 << 20, transcendentals=0),
        name="leaf_far",
    )(info, src, *coefs, mat, tb, near)


def pick_kernel(*refs):
    rings, out, sem = refs[:16], refs[16], refs[17]
    pairs = []
    for s in range(8):
        for h in range(2):
            for k in range(2):
                q = 4 * s + 2 * h + k
                pairs.append((rings[2 * s + h].at[pl.ds(288 * k + 256, 32)], out.at[pl.ds(32 * q, 32)]))
    for c in copies_of(pairs, sem):
        c.wait()


def pick_tops(rings):
    return pl.pallas_call(
        pick_kernel,
        in_specs=[pl.BlockSpec(memory_space=pl.ANY)] * 16,
        out_specs=pl.BlockSpec(memory_space=VMEM),
        out_shape=VMEM((1024, 128), BF),
        scratch_shapes=[pltpu.SemaphoreType.DMA((32,))],
        compiler_params=pltpu.CompilerParams(vmem_limit_bytes=SMALL),
        cost_estimate=pl.CostEstimate(flops=0, bytes_accessed=1 << 20, transcendentals=0),
        name="pick_tops",
    )(*rings)


def join_kernel(a, b, c, d, out, sem):
    n = a.shape[0]
    for copy in copies_of([(r, out.at[pl.ds(k * n, n)]) for k, r in enumerate((a, b, c, d))], sem):
        copy.wait()


def join(arrays):
    return pl.pallas_call(
        join_kernel,
        in_specs=[pl.BlockSpec(memory_space=pl.ANY)] * 4,
        out_specs=pl.BlockSpec(memory_space=VMEM),
        out_shape=VMEM((4096, 128), BF),
        scratch_shapes=[pltpu.SemaphoreType.DMA((4,))],
        compiler_params=pltpu.CompilerParams(vmem_limit_bytes=SMALL),
        cost_estimate=pl.CostEstimate(flops=0, bytes_accessed=2 << 20, transcendentals=0),
        name="join",
    )(*arrays)


def top_kernel(info, src, own, other, mat, out):
    x, core, z, y = info[1], info[2], info[3], info[4]
    acc = jnp.zeros((R, R), F32)
    rows = []
    for n in range(32):
        g = jnp.clip(src[0, n], 0, X * CORE * Z * Y - 1)
        sy = (y - g) & 3
        sz = (z - (g >> 2)) & 7
        sx = (x - (g >> 6)) & 3
        same = ((g >> 5) & 1) == core
        at = pl.ds(pl.multiple_of(((sx * Z + sz) * Y + sy) * 32, 32), 32)
        t = jnp.where(same, own[at, :], other[at, :])
        rows += [t[:, :R], t[:, R:]]
    for q in range(8):
        acc += dot(wide([mat[0, 4 * q + n] for n in range(4)]), jnp.concatenate(rows[8 * q : 8 * q + 8], axis=0))
    out[...] = acc.astype(BF)


def top_far(info, src, own, other, mat):
    v = pl.BlockSpec(memory_space=VMEM)
    s = pl.BlockSpec(memory_space=pltpu.SMEM)
    return pl.pallas_call(
        top_kernel,
        in_specs=[s, s, v, v, v],
        out_specs=v,
        out_shape=jax.ShapeDtypeStruct((R, R), BF),
        compiler_params=pltpu.CompilerParams(vmem_limit_bytes=SMALL),
        cost_estimate=pl.CostEstimate(flops=32 * 2 * R**3, bytes_accessed=3 << 20, transcendentals=0),
        name="top_far",
    )(info, src, own, other, mat)


def mid_kernel(info, src, mat, *refs):
    rings, (out, raw, mv, mask, sem) = refs[:16], refs[16:]
    z, y = info[3], info[4]
    copies = copies_of([(rings[s], raw.at[s]) for s in range(16)], sem)
    copies += copies_of(parts(mat, mv, 8), sem.at[pl.ds(16, 8)])
    half_masks(mask)
    for c in copies:
        c.wait()
    done = []
    for p in range(8):
        acc = jnp.zeros((R, 2 * R), F32)
        for n in range(16):
            g = jnp.clip(src[p, n] - info[5], 0, Z * Y * 8 - 1)
            sy = (y - (g >> 3)) & 3
            sz = (z - (g >> 5)) & 7
            at = (sy & 1) * 288 + ((g >> 1) & 3) * R
            t = raw[sz * 2 + (sy >> 1), pl.ds(pl.multiple_of(at, 32), R), :]
            acc += dot(mv[p, n], t * mask[g & 1])
        done.append(fold(acc))
    for p in range(8):
        out[p] = done[p]


def mid_far(info, src, mat, rings):
    v = pl.BlockSpec(memory_space=VMEM)
    s = pl.BlockSpec(memory_space=pltpu.SMEM)
    return pl.pallas_call(
        mid_kernel,
        in_specs=[s, s] + [pl.BlockSpec(memory_space=pl.ANY)] * 17,
        out_specs=v,
        out_shape=VMEM((8, R, R), F32),
        scratch_shapes=[
            VMEM((16, 576, 128), BF), VMEM(mat.shape, BF), VMEM((3, R, 2 * R), BF), pltpu.SemaphoreType.DMA((24,)),
        ],
        compiler_params=pltpu.CompilerParams(vmem_limit_bytes=12 << 20),
        cost_estimate=pl.CostEstimate(flops=128 * 2 * R**3, bytes_accessed=6 << 20, transcendentals=0),
        name="mid_far",
    )(info, src, mat, *rings)


def tail_kernel(top_ref, far, down, base, both, out, buf, sem):
    top = top_ref[...]
    local = [(far[p] + dot(down[p], top)).astype(BF) for p in range(8)]
    copies = []
    for p in range(8):
        at = pl.ds(8 * p, 8)
        res = dot(both[at].reshape(8 * R, R), local[p]).reshape(8, R, R)
        buf[at] = (base[at] + res).astype(BF)
        copies.append(pltpu.make_async_copy(buf.at[at], out.at[at], sem.at[p]))
        copies[-1].start()
    for c in copies:
        c.wait()


def tail(top, far, down, base, both):
    v = pl.BlockSpec(memory_space=VMEM)
    return pl.pallas_call(
        tail_kernel,
        in_specs=[v] * 5,
        out_specs=pl.BlockSpec(memory_space=pltpu.HBM),
        out_shape=jax.ShapeDtypeStruct((64, R, R), BF),
        scratch_shapes=[VMEM((64, R, R), BF), pltpu.SemaphoreType.DMA((8,))],
        compiler_params=pltpu.CompilerParams(vmem_limit_bytes=SMALL),
        cost_estimate=pl.CostEstimate(flops=72 * 2 * R**3, bytes_accessed=6 << 20, transcendentals=0),
        name="tail",
    )(top, far, down, base, both)


def place(d):
    return d // (CORE * Z * Y), d // (Z * Y) % CORE, d // Y % Z, d % Y


def index(x, c, z, y):
    return ((x % X * CORE + c % CORE) * Z + z % Z) * Y + y % Y


def shift(a, x=0, c=0, z=0, y=0):
    pairs = []
    for d in range(X * CORE * Z * Y):
        px, pc, pz, py = place(d)
        pairs.append((d, index(px + x, pc + c, pz + z, py + y)))
    return lax.ppermute(a, BOTH, pairs)


def some(a, pairs):
    return lax.ppermute(a, BOTH, pairs)


def halo(a):
    n = X * CORE * Z * Y
    up = [(i, i + 1) for i in range(n - 1)]
    return some(a, up), some(a, [(j, i) for i, j in up])


def tie(*arrays):
    return lax.optimization_barrier(arrays)


def shards(
    charges,
    source_basis,
    target_basis,
    leaf_up,
    mid_up,
    leaf_down,
    mid_down,
    leaf_far_src,
    leaf_far_mat,
    mid_far_src,
    mid_far_mat,
    top_far_src,
    top_far_mat,
    near_src,
    near_count,
    near_mat,
):
    me = lax.axis_index(BOTH).astype(jnp.int32)
    px, pc, pz, py = place(me)
    info = jnp.stack([(me - 1) * 64, px, pc, pz, py, me // (Z * Y) * (Z * Y * 8)])

    packed, coef, mt = upsweep(charges, source_basis, leaf_up, mid_up)

    m1, m3, m2 = shift(mt, y=1), shift(mt, y=-1), shift(mt, y=2)
    rings = {(0, 0): jnp.concatenate([mt, m1], axis=0), (0, 1): jnp.concatenate([m2, m3], axis=0)}
    for s in range(1, 4):
        for h in range(2):
            rings[s, h] = shift(rings[s - 1, h], z=1)
            rings[8 - s, h] = shift(rings[(9 - s) % 8, h], z=-1)
    rings[4, 0] = shift(rings[3, 0], z=1)
    rings[4, 1] = shift(rings[5, 1], z=-1)
    rings = [rings[s, h] for s in range(8) for h in range(2)]

    all_z = pick_tops(rings)
    all_z, rings[0], packed = tie(all_z, rings[0], packed)
    by_x = [all_z] + [shift(all_z, x=s) for s in range(1, X)]
    before, after = halo(packed)
    far = mid_far(info, mid_far_src, mid_far_mat, rings)
    *by_x, coef, packed, far = tie(*by_x, coef, packed, far)
    all_x = join(by_x)
    other = shift(all_x, c=1)
    coef_before, coef_after = halo(coef)
    near, far_v, tb_v, both = near_field(
        info, near_src.T, near_count, (before, packed, after), near_mat, leaf_far_mat, target_basis, leaf_down
    )
    base = leaf_far(info, leaf_far_src.T, (coef_before, coef, coef_after), far_v, tb_v, near)
    top_local = top_far(info, top_far_src, all_x, other, top_far_mat)
    return tail(top_local, far, mid_down, base, both)


def solution(mesh):
    row = P(BOTH, None)
    three = P(BOTH, None, None)
    four = P(BOTH, None, None, None)
    in_specs = (
        three, three, three, three, three, three, three,
        row, four, row, four, row, four, row, P(BOTH), four,
    )
    return jax.shard_map(shards, mesh=mesh, in_specs=in_specs, out_specs=three, check_vma=False)
```

time: 127 us -> 110 us (0.87)
  local copies, waits for them, and re-layouts: 17.8 us -> 4.75 us
  waiting for transfers between devices: 11.6 us -> 21.7 us
  Pallas kernels: 37.2 us -> 30.4 us
  starting transfers between devices: 59 us -> 52.6 us
    unnamed x72 -> x24, local copies, waits for them, and re-layouts: 16.3 us -> 4.64 us
    pallas_call x3 -> x6, Pallas kernels: 33.4 us -> 24.5 us  [the longest x1 9.03 us: near_field(): pl.pallas_call(near_kernel, in_specs=[s] * 3 + [pl.BlockSpec(memory_space...]
    ppermute x4, waiting for transfers between devices: 4.06 us -> 9.53 us  [some(): return lax.ppermute(a, BOTH, pairs)]
    ppermute x22 -> x21, waiting for transfers between devices: 7.57 us -> 12.2 us  [shift(): return lax.ppermute(a, BOTH, pairs)]
    ppermute x22 -> x21, starting transfers between devices: 40.6 us -> 37 us  [shift(): return lax.ppermute(a, BOTH, pairs)]
    ppermute x4, starting transfers between devices: 18.5 us -> 15.6 us  [some(): return lax.ppermute(a, BOTH, pairs)]
    pallas_call x1, Pallas kernels: 2.19 us -> 4.83 us  [upsweep(): pl.pallas_call(up_kernel, grid=(4,), in_specs=[leaf, leaf, leaf, pl.Block...]
    slice x6 -> x0, local copies, waits for them, and re-layouts: 1.35 us -> none  [the longest x2 1.32 us: shards(): f4, b4 = (shift(f3[:512], z=1), shift(b3[512:], z=-1))]
  transfers between devices with their start and end apart: 26 -> 25, of which waited for: 5 -> 10; matrix products, arithmetic and copies ran while one was open for 1% -> 1% of each run, Pallas kernels for 20% -> 19%
where the time goes in v2:
time: 110 us
  starting transfers between devices  52.6 us (48%)
  Pallas kernels  30.4 us (28%)
  waiting for transfers between devices  21.7 us (20%)
  local copies, waits for them, and re-layouts  4.75 us (4%)
    ppermute x21, starting transfers between devices, shift(): return lax.ppermute(a, BOTH, pairs)  37 us
    ppermute x4, starting transfers between devices, some(): return lax.ppermute(a, BOTH, pairs)  15.6 us
    ppermute x21, waiting for transfers between devices, shift(): return lax.ppermute(a, BOTH, pairs)  12.2 us
    ppermute x4, waiting for transfers between devices, some(): return lax.ppermute(a, BOTH, pairs)  9.53 us
    pallas_call x1, Pallas kernels, near_field(): pl.pallas_call(near_kernel, in_specs=[s] * 3 + [pl.BlockSpec(memory_space...  9.03 us
    pallas_call x1, Pallas kernels, leaf_far(): pl.pallas_call(far_kernel, in_specs=[s] * 2 + [pl.BlockSpec(memory_space=...  6.84 us
    pallas_call x1, Pallas kernels, mid_far(): pl.pallas_call(mid_kernel, in_specs=[s, s] + [pl.BlockSpec(memory_space=p...  5.46 us
    pallas_call x1, Pallas kernels, upsweep(): pl.pallas_call(up_kernel, grid=(4,), in_specs=[leaf, leaf, leaf, pl.Block...  4.83 us
  transfers between devices with their start and end apart: 25, of which 10 were waited for; matrix products, arithmetic and copies ran while one was open for 1% of the time, Pallas kernels for 19%

profile of v2, /device:TPU:1, one launch (start us, length us, event | category | flops | bytes accessed | tf_op | source)
XLA Modules:
  0.0 109.8 jit_solution(2169076293642237373)
XLA Ops:
  0.0 4.8 %upsweep.1 = (bf16[32,64,128]{2,1,0:T(8,128)(2,1)}, bf16[32,64,128]{2,1,0:T(8,128)(2,1)}, bf16[288,128]{1,0:T(8,128)(2,1)}) custom-call(bf16[64,64,64]{2,1,0:T(8,128)(2,1)} %c_ref.1, bf16[64,64,64]{2,1,0:T(8,128)(2,1)} %s_ref.1, bf16[64,64,64]{2,1,0:T(8,128)(2,1)} %lu_ref.1, bf16[8,64,64]{2,1,0:T(8,128)(2,1)} %mu_ref.1), custom_call_target="tpu_custom_call" | custom-call | flops 71303168 | bytes 5242880 | tf_op jit(solution)/shard_map/upsweep/pallas_call | solution.py:63
  4.8 3.6 %collective-permute-start.2 = (bf16[288,128]{1,0:T(8,128)(2,1)}, bf16[288,128]{1,0:T(8,128)(2,1)S(1)}, u32[]{:S(2)}, u32[]{:S(2)}) collective-permute-start(bf16[288,128]{1,0:T(8,128)(2,1)} %get-tuple-element.22), channel_id=1, source_target_pairs={{0,3},{1,0},{2,1},{3,2},{4,7},{5,4},{6,5},{7,6},{8,11},{9,8},{10,9... | collective-permute-start | bytes 221192 | tf_op jit(solution)/shard_map/ppermute | solution.py:375
  10.5 4.1 %collective-permute-done = bf16[288,128]{1,0:T(8,128)(2,1)S(1)} collective-permute-done((bf16[288,128]{1,0:T(8,128)(2,1)}, bf16[288,128]{1,0:T(8,128)(2,1)S(1)}, u32[]{:S(2)}, u32[]{:S(2)}) %collective-permute-start) | collective-permute-done | bytes 73760 | tf_op jit(solution)/shard_map/ppermute | solution.py:375
  14.6 1.7 %collective-permute-start.3 = (bf16[576,128]{1,0:T(8,128)(2,1)S(1)}, bf16[576,128]{1,0:T(8,128)(2,1)S(1)}, u32[]{:S(2)}, u32[]{:S(2)}) collective-permute-start(bf16[576,128]{1,0:T(8,128)(2,1)S(1)} %constant_dynamic-update-slice_fusion.refs_0_), channel_id=1, source_target_pairs={{0,4},{1,5},{2,6},{3,7},{4,8},{5,9},{6,10},{7,11},{8,12},{9,13},{1... | collective-permute-start | bytes 442376 | tf_op jit(solution)/shard_map/ppermute | solution.py:375
  16.4 4.0 %collective-permute-start.10 = (bf16[576,128]{1,0:T(8,128)(2,1)S(1)}, bf16[576,128]{1,0:T(8,128)(2,1)S(1)}, u32[]{:S(2)}, u32[]{:S(2)}) collective-permute-start(bf16[576,128]{1,0:T(8,128)(2,1)S(1)} %constant_dynamic-update-slice_fusion.2.refs_1_), channel_id=1, source_target_pairs={{0,28},{1,29},{2,30},{3,31},{4,0},{5,1},{6,2},{7,3},{8,4},{9,5},{1... | collective-permute-start | bytes 442376 | tf_op jit(solution)/shard_map/ppermute | solution.py:375
  22.8 2.8 %collective-permute-start.11 = (bf16[576,128]{1,0:T(8,128)(2,1)S(1)}, bf16[576,128]{1,0:T(8,128)(2,1)S(1)}, u32[]{:S(2)}, u32[]{:S(2)}) collective-permute-start(bf16[576,128]{1,0:T(8,128)(2,1)S(1)} %collective-permute-done.10.refs_15_), channel_id=1, source_target_pairs={{0,28},{1,29},{2,30},{3,31},{4,0},{5,1},{6,2},{7,3},{8,4},{9,5},{1... | collective-permute-start | bytes 442376 | tf_op jit(solution)/shard_map/ppermute | solution.py:375
  25.6 2.6 %collective-permute-start.15 = (bf16[576,128]{1,0:T(8,128)(2,1)S(1)}, bf16[576,128]{1,0:T(8,128)(2,1)S(1)}, u32[]{:S(2)}, u32[]{:S(2)}) collective-permute-start(bf16[576,128]{1,0:T(8,128)(2,1)S(1)} %collective-permute-done.14.refs_14_), channel_id=1, source_target_pairs={{0,28},{1,29},{2,30},{3,31},{4,0},{5,1},{6,2},{7,3},{8,4},{9,5},{1... | collective-permute-start | bytes 442376 | tf_op jit(solution)/shard_map/ppermute | solution.py:375
  28.8 3.1 %collective-permute-start.12 = (bf16[576,128]{1,0:T(8,128)(2,1)S(1)}, bf16[576,128]{1,0:T(8,128)(2,1)S(1)}, u32[]{:S(2)}, u32[]{:S(2)}) collective-permute-start(bf16[576,128]{1,0:T(8,128)(2,1)S(1)} %collective-permute-done.11.refs_13_), channel_id=1, source_target_pairs={{0,28},{1,29},{2,30},{3,31},{4,0},{5,1},{6,2},{7,3},{8,4},{9,5},{1... | collective-permute-start | bytes 442376 | tf_op jit(solution)/shard_map/ppermute | solution.py:375
  31.9 1.6 %collective-permute-start.16 = (bf16[576,128]{1,0:T(8,128)(2,1)S(1)}, bf16[576,128]{1,0:T(8,128)(2,1)S(1)}, u32[]{:S(2)}, u32[]{:S(2)}) collective-permute-start(bf16[576,128]{1,0:T(8,128)(2,1)S(1)} %collective-permute-done.15.refs_12_), channel_id=1, source_target_pairs={{0,28},{1,29},{2,30},{3,31},{4,0},{5,1},{6,2},{7,3},{8,4},{9,5},{1... | collective-permute-start | bytes 442376 | tf_op jit(solution)/shard_map/ppermute | solution.py:375
  33.5 1.5 %collective-permute-done.7.refs_6_ = bf16[576,128]{1,0:T(8,128)(2,1)S(1)} collective-permute-done((bf16[576,128]{1,0:T(8,128)(2,1)S(1)}, bf16[576,128]{1,0:T(8,128)(2,1)S(1)}, u32[]{:S(2)}, u32[]{:S(2)}) %collective-permute-start.7) | collective-permute-done | bytes 147488 | tf_op jit(solution)/shard_map/ppermute | solution.py:375
  35.1 3.4 %collective-permute-start.13 = (bf16[576,128]{1,0:T(8,128)(2,1)S(1)}, bf16[576,128]{1,0:T(8,128)(2,1)S(1)}, u32[]{:S(2)}, u32[]{:S(2)}) collective-permute-start(bf16[576,128]{1,0:T(8,128)(2,1)S(1)} %collective-permute-done.12.refs_11_), channel_id=1, source_target_pairs={{0,28},{1,29},{2,30},{3,31},{4,0},{5,1},{6,2},{7,3},{8,4},{9,5},{1... | collective-permute-start | bytes 442376 | tf_op jit(solution)/shard_map/ppermute | solution.py:375
  38.5 2.1 %collective-permute-done.8.refs_7_ = bf16[576,128]{1,0:T(8,128)(2,1)S(1)} collective-permute-done((bf16[576,128]{1,0:T(8,128)(2,1)S(1)}, bf16[576,128]{1,0:T(8,128)(2,1)S(1)}, u32[]{:S(2)}, u32[]{:S(2)}) %collective-permute-start.8) | collective-permute-done | bytes 147488 | tf_op jit(solution)/shard_map/ppermute | solution.py:375
  40.5 2.2 %collective-permute-done.9.refs_8_ = bf16[576,128]{1,0:T(8,128)(2,1)S(1)} collective-permute-done((bf16[576,128]{1,0:T(8,128)(2,1)S(1)}, bf16[576,128]{1,0:T(8,128)(2,1)S(1)}, u32[]{:S(2)}, u32[]{:S(2)}) %collective-permute-start.9) | collective-permute-done | bytes 147488 | tf_op jit(solution)/shard_map/ppermute | solution.py:375
  43.5 2.6 %collective-permute-start.19 = (bf16[1024,128]{1,0:T(8,128)(2,1)S(1)}, bf16[1024,128]{1,0:T(8,128)(2,1)S(1)}, u32[]{:S(2)}, u32[]{:S(2)}) collective-permute-start(bf16[1024,128]{1,0:T(8,128)(2,1)S(1)} %pick_tops.1.a), channel_id=1, source_target_pairs={{0,192},{1,193},{2,194},{3,195},{4,196},{5,197},{6,198},{7,199},{8... | collective-permute-start | bytes 786440 | tf_op jit(solution)/shard_map/ppermute | solution.py:375
  47.2 1.6 %copy-done = bf16[8,16,64,64]{3,2,1,0:T(8,128)(2,1)S(1)} copy-done((bf16[8,16,64,64]{3,2,1,0:T(8,128)(2,1)S(1)}, bf16[8,16,64,64]{3,2,1,0:T(8,128)(2,1)}, u32[]{:S(2)}) %copy-start) | copy-done | bytes 1048600
  49.5 5.5 %mid_far.1.far = f32[8,64,64]{2,1,0:T(8,128)S(1)} custom-call(s32[6]{0:T(128)S(1)} %stack.27.info, s32[8,16]{1,0:T(8,128)S(1)} %copy-done.7, bf16[8,16,64,64]{3,2,1,0:T(8,128)(2,1)S(1)} %copy-done, bf16[576,128]{1,0:T(8,128)(2,1)S(1)} %constant_dynamic-update-slice_fusion.refs_0_, bf16[576,128]{1,0:T(8,128)(2,1)S(1)} %constant_dynamic-update-slice_fusion.2.refs_1_, ...), custom_call_target="tpu_custom_call" | custom-call | flops 67108864 | bytes 6291456 | tf_op jit(solution)/shard_map/mid_far/pallas_call | solution.py:320
  56.8 7.9 %collective-permute-start.20 = (bf16[4096,128]{1,0:T(8,128)(2,1)S(1)}, bf16[4096,128]{1,0:T(8,128)(2,1)S(1)}, u32[]{:S(2)}, u32[]{:S(2)}) collective-permute-start(bf16[4096,128]{1,0:T(8,128)(2,1)S(1)} %join.1.own), channel_id=1, source_target_pairs={{0,32},{1,33},{2,34},{3,35},{4,36},{5,37},{6,38},{7,39},{8,40},{9,... | collective-permute-start | bytes 3145736 | tf_op jit(solution)/shard_map/ppermute | solution.py:375
  64.7 4.8 %collective-permute-start.24 = (bf16[32,64,128]{2,1,0:T(8,128)(2,1)}, bf16[32,64,128]{2,1,0:T(8,128)(2,1)S(1)}, u32[]{:S(2)}, u32[]{:S(2)}) collective-permute-start(bf16[32,64,128]{2,1,0:T(8,128)(2,1)} %get-tuple-element.34.co), channel_id=1, source_target_pairs={{1,0},{2,1},{3,2},{4,3},{5,4},{6,5},{7,6},{8,7},{9,8},{10,9},{11,1... | collective-permute-start | bytes 1572872 | tf_op jit(solution)/shard_map/ppermute | solution.py:379
  69.5 1.9 %collective-permute-start.23 = (bf16[32,64,128]{2,1,0:T(8,128)(2,1)}, bf16[32,64,128]{2,1,0:T(8,128)(2,1)S(1)}, u32[]{:S(2)}, u32[]{:S(2)}) collective-permute-start(bf16[32,64,128]{2,1,0:T(8,128)(2,1)} %get-tuple-element.34.co), channel_id=1, source_target_pairs={{0,1},{1,2},{2,3},{3,4},{4,5},{5,6},{6,7},{7,8},{8,9},{9,10},{10,1... | collective-permute-start | bytes 1572872 | tf_op jit(solution)/shard_map/ppermute | solution.py:379
  71.4 7.0 %collective-permute-start.22 = (bf16[32,64,128]{2,1,0:T(8,128)(2,1)S(1)}, bf16[32,64,128]{2,1,0:T(8,128)(2,1)S(1)}, u32[]{:S(2)}, u32[]{:S(2)}) collective-permute-start(bf16[32,64,128]{2,1,0:T(8,128)(2,1)S(1)} %copy-done.2), channel_id=1, source_target_pairs={{1,0},{2,1},{3,2},{4,3},{5,4},{6,5},{7,6},{8,7},{9,8},{10,9},{11,1... | collective-permute-start | bytes 1572872 | tf_op jit(solution)/shard_map/ppermute | solution.py:379
  78.4 1.9 %collective-permute-start.21 = (bf16[32,64,128]{2,1,0:T(8,128)(2,1)S(1)}, bf16[32,64,128]{2,1,0:T(8,128)(2,1)S(1)}, u32[]{:S(2)}, u32[]{:S(2)}) collective-permute-start(bf16[32,64,128]{2,1,0:T(8,128)(2,1)S(1)} %copy-done.2), channel_id=1, source_target_pairs={{0,1},{1,2},{2,3},{3,4},{4,5},{5,6},{6,7},{7,8},{8,9},{9,10},{10,1... | collective-permute-start | bytes 1572872 | tf_op jit(solution)/shard_map/ppermute | solution.py:379
  80.3 8.1 %collective-permute-done.23.cb = bf16[32,64,128]{2,1,0:T(8,128)(2,1)S(1)} collective-permute-done((bf16[32,64,128]{2,1,0:T(8,128)(2,1)}, bf16[32,64,128]{2,1,0:T(8,128)(2,1)S(1)}, u32[]{:S(2)}, u32[]{:S(2)}) %collective-permute-start.23) | collective-permute-done | bytes 524320 | tf_op jit(solution)/shard_map/ppermute | solution.py:379
  89.3 9.0 %near.1 = (f32[64,64,64]{2,1,0:T(8,128)S(1)}, bf16[64,8,64,64]{3,2,1,0:T(8,128)(2,1)S(1)}, bf16[64,64,64]{2,1,0:T(8,128)(2,1)S(1)}, bf16[64,64,64]{2,1,0:T(8,128)(2,1)S(1)}) custom-call(s32[6]{0:T(128)} %copy-done.4, s32[8,64]{1,0:T(8,128)} %bitcast.9, s32[64]{0:T(128)} %cnt.1, bf16[32,64,128]{2,1,0:T(8,128)(2,1)} %copy-done.10, ...), custom_call_target="tpu_custom_call" | custom-call | flops 301989888 | bytes 25165824 | tf_op jit(solution)/shard_map/near/pallas_call | solution.py:149
  100.3 6.8 %leaf_far.1.base = f32[64,64,64]{2,1,0:T(8,128)S(1)} custom-call(s32[6]{0:T(128)S(1)} %copy-done.5, s32[8,64]{1,0:T(8,128)S(1)} %bitcast.8, bf16[32,64,128]{2,1,0:T(8,128)(2,1)S(1)} %collective-permute-done.21.ku, bf16[32,64,128]{2,1,0:T(8,128)(2,1)S(1)} %copy-done.2, bf16[32,64,128]{2,1,0:T(8,128)(2,1)S(1)} %collective-permute-done.22.kd, ...), custom_call_target="tpu_custom_call" | custom-call | flops 301989888 | bytes 16777216 | tf_op jit(solution)/shard_map/leaf_far/pallas_call | solution.py:201
  (61 shorter events, 14.6 us)
Async XLA Ops:
  4.8 11.5 %collective-permute-start.2 = (bf16[288,128]{1,0:T(8,128)(2,1)}, bf16[288,128]{1,0:T(8,128)(2,1)S(1)}, u32[]{:S(2)}, u32[]{:S(2)}) collective-permute-start(bf16[288,128]{1,0:T(8,128)(2,1)} %get-tuple-element.22), channel_id=1, source_target_pairs={{0,3},{1,0},{2,1},{3,2},{4,7},{5,4},{6,5},{7,6},{8,11},{9,8},{10,9... | collective-permute-start | bytes 221192 | tf_op jit(solution)/shard_map/ppermute | solution.py:375
  8.5 7.8 %collective-permute-start.1 = (bf16[288,128]{1,0:T(8,128)(2,1)}, bf16[288,128]{1,0:T(8,128)(2,1)S(1)}, u32[]{:S(2)}, u32[]{:S(2)}) collective-permute-start(bf16[288,128]{1,0:T(8,128)(2,1)} %get-tuple-element.22), channel_id=1, source_target_pairs={{0,2},{1,3},{2,0},{3,1},{4,6},{5,7},{6,4},{7,5},{8,10},{9,11},{10,... | collective-permute-start | bytes 221192 | tf_op jit(solution)/shard_map/ppermute | solution.py:375
  8.8 5.8 %collective-permute-start = (bf16[288,128]{1,0:T(8,128)(2,1)}, bf16[288,128]{1,0:T(8,128)(2,1)S(1)}, u32[]{:S(2)}, u32[]{:S(2)}) collective-permute-start(bf16[288,128]{1,0:T(8,128)(2,1)} %get-tuple-element.22), channel_id=1, source_target_pairs={{0,1},{1,2},{2,3},{3,0},{4,5},{5,6},{6,7},{7,4},{8,9},{9,10},{10,1... | collective-permute-start | bytes 221192 | tf_op jit(solution)/shard_map/ppermute | solution.py:375
  14.6 8.2 %collective-permute-start.3 = (bf16[576,128]{1,0:T(8,128)(2,1)S(1)}, bf16[576,128]{1,0:T(8,128)(2,1)S(1)}, u32[]{:S(2)}, u32[]{:S(2)}) collective-permute-start(bf16[576,128]{1,0:T(8,128)(2,1)S(1)} %constant_dynamic-update-slice_fusion.refs_0_), channel_id=1, source_target_pairs={{0,4},{1,5},{2,6},{3,7},{4,8},{5,9},{6,10},{7,11},{8,12},{9,13},{1... | collective-permute-start | bytes 442376 | tf_op jit(solution)/shard_map/ppermute | solution.py:375
  16.4 6.4 %collective-permute-start.10 = (bf16[576,128]{1,0:T(8,128)(2,1)S(1)}, bf16[576,128]{1,0:T(8,128)(2,1)S(1)}, u32[]{:S(2)}, u32[]{:S(2)}) collective-permute-start(bf16[576,128]{1,0:T(8,128)(2,1)S(1)} %constant_dynamic-update-slice_fusion.2.refs_1_), channel_id=1, source_target_pairs={{0,28},{1,29},{2,30},{3,31},{4,0},{5,1},{6,2},{7,3},{8,4},{9,5},{1... | collective-permute-start | bytes 442376 | tf_op jit(solution)/shard_map/ppermute | solution.py:375
  21.9 6.4 %collective-permute-start.4 = (bf16[576,128]{1,0:T(8,128)(2,1)S(1)}, bf16[576,128]{1,0:T(8,128)(2,1)S(1)}, u32[]{:S(2)}, u32[]{:S(2)}) collective-permute-start(bf16[576,128]{1,0:T(8,128)(2,1)S(1)} %constant_dynamic-update-slice_fusion.2.refs_1_), channel_id=1, source_target_pairs={{0,4},{1,5},{2,6},{3,7},{4,8},{5,9},{6,10},{7,11},{8,12},{9,13},{1... | collective-permute-start | bytes 442376 | tf_op jit(solution)/shard_map/ppermute | solution.py:375
  22.8 5.8 %collective-permute-start.5 = (bf16[576,128]{1,0:T(8,128)(2,1)S(1)}, bf16[576,128]{1,0:T(8,128)(2,1)S(1)}, u32[]{:S(2)}, u32[]{:S(2)}) collective-permute-start(bf16[576,128]{1,0:T(8,128)(2,1)S(1)} %collective-permute-done.3.refs_2_), channel_id=1, source_target_pairs={{0,4},{1,5},{2,6},{3,7},{4,8},{5,9},{6,10},{7,11},{8,12},{9,13},{1... | collective-permute-start | bytes 442376 | tf_op jit(solution)/shard_map/ppermute | solution.py:375
  22.8 6.0 %collective-permute-start.11 = (bf16[576,128]{1,0:T(8,128)(2,1)S(1)}, bf16[576,128]{1,0:T(8,128)(2,1)S(1)}, u32[]{:S(2)}, u32[]{:S(2)}) collective-permute-start(bf16[576,128]{1,0:T(8,128)(2,1)S(1)} %collective-permute-done.10.refs_15_), channel_id=1, source_target_pairs={{0,28},{1,29},{2,30},{3,31},{4,0},{5,1},{6,2},{7,3},{8,4},{9,5},{1... | collective-permute-start | bytes 442376 | tf_op jit(solution)/shard_map/ppermute | solution.py:375
  25.6 6.3 %collective-permute-start.15 = (bf16[576,128]{1,0:T(8,128)(2,1)S(1)}, bf16[576,128]{1,0:T(8,128)(2,1)S(1)}, u32[]{:S(2)}, u32[]{:S(2)}) collective-permute-start(bf16[576,128]{1,0:T(8,128)(2,1)S(1)} %collective-permute-done.14.refs_14_), channel_id=1, source_target_pairs={{0,28},{1,29},{2,30},{3,31},{4,0},{5,1},{6,2},{7,3},{8,4},{9,5},{1... | collective-permute-start | bytes 442376 | tf_op jit(solution)/shard_map/ppermute | solution.py:375
  28.3 5.3 %collective-permute-start.6 = (bf16[576,128]{1,0:T(8,128)(2,1)S(1)}, bf16[576,128]{1,0:T(8,128)(2,1)S(1)}, u32[]{:S(2)}, u32[]{:S(2)}) collective-permute-start(bf16[576,128]{1,0:T(8,128)(2,1)S(1)} %collective-permute-done.4.refs_3_), channel_id=1, source_target_pairs={{0,4},{1,5},{2,6},{3,7},{4,8},{5,9},{6,10},{7,11},{8,12},{9,13},{1... | collective-permute-start | bytes 442376 | tf_op jit(solution)/shard_map/ppermute | solution.py:375
  28.6 6.4 %collective-permute-start.7 = (bf16[576,128]{1,0:T(8,128)(2,1)S(1)}, bf16[576,128]{1,0:T(8,128)(2,1)S(1)}, u32[]{:S(2)}, u32[]{:S(2)}) collective-permute-start(bf16[576,128]{1,0:T(8,128)(2,1)S(1)} %collective-permute-done.5.refs_4_), channel_id=1, source_target_pairs={{0,4},{1,5},{2,6},{3,7},{4,8},{5,9},{6,10},{7,11},{8,12},{9,13},{1... | collective-permute-start | bytes 442376 | tf_op jit(solution)/shard_map/ppermute | solution.py:375
  28.8 6.2 %collective-permute-start.12 = (bf16[576,128]{1,0:T(8,128)(2,1)S(1)}, bf16[576,128]{1,0:T(8,128)(2,1)S(1)}, u32[]{:S(2)}, u32[]{:S(2)}) collective-permute-start(bf16[576,128]{1,0:T(8,128)(2,1)S(1)} %collective-permute-done.11.refs_13_), channel_id=1, source_target_pairs={{0,28},{1,29},{2,30},{3,31},{4,0},{5,1},{6,2},{7,3},{8,4},{9,5},{1... | collective-permute-start | bytes 442376 | tf_op jit(solution)/shard_map/ppermute | solution.py:375
  31.9 6.5 %collective-permute-start.16 = (bf16[576,128]{1,0:T(8,128)(2,1)S(1)}, bf16[576,128]{1,0:T(8,128)(2,1)S(1)}, u32[]{:S(2)}, u32[]{:S(2)}) collective-permute-start(bf16[576,128]{1,0:T(8,128)(2,1)S(1)} %collective-permute-done.15.refs_12_), channel_id=1, source_target_pairs={{0,28},{1,29},{2,30},{3,31},{4,0},{5,1},{6,2},{7,3},{8,4},{9,5},{1... | collective-permute-start | bytes 442376 | tf_op jit(solution)/shard_map/ppermute | solution.py:375
  33.5 7.0 %collective-permute-start.8 = (bf16[576,128]{1,0:T(8,128)(2,1)S(1)}, bf16[576,128]{1,0:T(8,128)(2,1)S(1)}, u32[]{:S(2)}, u32[]{:S(2)}) collective-permute-start(bf16[576,128]{1,0:T(8,128)(2,1)S(1)} %collective-permute-done.6.refs_5_), channel_id=1, source_target_pairs={{0,4},{1,5},{2,6},{3,7},{4,8},{5,9},{6,10},{7,11},{8,12},{9,13},{1... | collective-permute-start | bytes 442376 | tf_op jit(solution)/shard_map/ppermute | solution.py:375
  35.0 7.7 %collective-permute-start.9 = (bf16[576,128]{1,0:T(8,128)(2,1)S(1)}, bf16[576,128]{1,0:T(8,128)(2,1)S(1)}, u32[]{:S(2)}, u32[]{:S(2)}) collective-permute-start(bf16[576,128]{1,0:T(8,128)(2,1)S(1)} %collective-permute-done.7.refs_6_), channel_id=1, source_target_pairs={{0,4},{1,5},{2,6},{3,7},{4,8},{5,9},{6,10},{7,11},{8,12},{9,13},{1... | collective-permute-start | bytes 442376 | tf_op jit(solution)/shard_map/ppermute | solution.py:375
  35.1 7.7 %collective-permute-start.13 = (bf16[576,128]{1,0:T(8,128)(2,1)S(1)}, bf16[576,128]{1,0:T(8,128)(2,1)S(1)}, u32[]{:S(2)}, u32[]{:S(2)}) collective-permute-start(bf16[576,128]{1,0:T(8,128)(2,1)S(1)} %collective-permute-done.12.refs_11_), channel_id=1, source_target_pairs={{0,28},{1,29},{2,30},{3,31},{4,0},{5,1},{6,2},{7,3},{8,4},{9,5},{1... | collective-permute-start | bytes 442376 | tf_op jit(solution)/shard_map/ppermute | solution.py:375
  43.5 11.5 %collective-permute-start.19 = (bf16[1024,128]{1,0:T(8,128)(2,1)S(1)}, bf16[1024,128]{1,0:T(8,128)(2,1)S(1)}, u32[]{:S(2)}, u32[]{:S(2)}) collective-permute-start(bf16[1024,128]{1,0:T(8,128)(2,1)S(1)} %pick_tops.1.a), channel_id=1, source_target_pairs={{0,192},{1,193},{2,194},{3,195},{4,196},{5,197},{6,198},{7,199},{8... | collective-permute-start | bytes 786440 | tf_op jit(solution)/shard_map/ppermute | solution.py:375
  46.0 9.0 %collective-permute-start.18 = (bf16[1024,128]{1,0:T(8,128)(2,1)S(1)}, bf16[1024,128]{1,0:T(8,128)(2,1)}, u32[]{:S(2)}, u32[]{:S(2)}) collective-permute-start(bf16[1024,128]{1,0:T(8,128)(2,1)S(1)} %pick_tops.1.a), channel_id=1, source_target_pairs={{0,128},{1,129},{2,130},{3,131},{4,132},{5,133},{6,134},{7,135},{8... | collective-permute-start | bytes 786440 | tf_op jit(solution)/shard_map/ppermute | solution.py:375
  46.6 9.1 %collective-permute-start.17 = (bf16[1024,128]{1,0:T(8,128)(2,1)S(1)}, bf16[1024,128]{1,0:T(8,128)(2,1)}, u32[]{:S(2)}, u32[]{:S(2)}) collective-permute-start(bf16[1024,128]{1,0:T(8,128)(2,1)S(1)} %pick_tops.1.a), channel_id=1, source_target_pairs={{0,64},{1,65},{2,66},{3,67},{4,68},{5,69},{6,70},{7,71},{8,72},{9,... | collective-permute-start | bytes 786440 | tf_op jit(solution)/shard_map/ppermute | solution.py:375
  56.8 50.4 %collective-permute-start.20 = (bf16[4096,128]{1,0:T(8,128)(2,1)S(1)}, bf16[4096,128]{1,0:T(8,128)(2,1)S(1)}, u32[]{:S(2)}, u32[]{:S(2)}) collective-permute-start(bf16[4096,128]{1,0:T(8,128)(2,1)S(1)} %join.1.own), channel_id=1, source_target_pairs={{0,32},{1,33},{2,34},{3,35},{4,36},{5,37},{6,38},{7,39},{8,40},{9,... | collective-permute-start | bytes 3145736 | tf_op jit(solution)/shard_map/ppermute | solution.py:375
  64.7 15.6 %collective-permute-start.24 = (bf16[32,64,128]{2,1,0:T(8,128)(2,1)}, bf16[32,64,128]{2,1,0:T(8,128)(2,1)S(1)}, u32[]{:S(2)}, u32[]{:S(2)}) collective-permute-start(bf16[32,64,128]{2,1,0:T(8,128)(2,1)} %get-tuple-element.34.co), channel_id=1, source_target_pairs={{1,0},{2,1},{3,2},{4,3},{5,4},{6,5},{7,6},{8,7},{9,8},{10,9},{11,1... | collective-permute-start | bytes 1572872 | tf_op jit(solution)/shard_map/ppermute | solution.py:379
  69.5 19.0 %collective-permute-start.23 = (bf16[32,64,128]{2,1,0:T(8,128)(2,1)}, bf16[32,64,128]{2,1,0:T(8,128)(2,1)S(1)}, u32[]{:S(2)}, u32[]{:S(2)}) collective-permute-start(bf16[32,64,128]{2,1,0:T(8,128)(2,1)} %get-tuple-element.34.co), channel_id=1, source_target_pairs={{0,1},{1,2},{2,3},{3,4},{4,5},{5,6},{6,7},{7,8},{8,9},{9,10},{10,1... | collective-permute-start | bytes 1572872 | tf_op jit(solution)/shard_map/ppermute | solution.py:379
  71.4 26.9 %collective-permute-start.22 = (bf16[32,64,128]{2,1,0:T(8,128)(2,1)S(1)}, bf16[32,64,128]{2,1,0:T(8,128)(2,1)S(1)}, u32[]{:S(2)}, u32[]{:S(2)}) collective-permute-start(bf16[32,64,128]{2,1,0:T(8,128)(2,1)S(1)} %copy-done.2), channel_id=1, source_target_pairs={{1,0},{2,1},{3,2},{4,3},{5,4},{6,5},{7,6},{8,7},{9,8},{10,9},{11,1... | collective-permute-start | bytes 1572872 | tf_op jit(solution)/shard_map/ppermute | solution.py:379
  78.4 21.3 %collective-permute-start.21 = (bf16[32,64,128]{2,1,0:T(8,128)(2,1)S(1)}, bf16[32,64,128]{2,1,0:T(8,128)(2,1)S(1)}, u32[]{:S(2)}, u32[]{:S(2)}) collective-permute-start(bf16[32,64,128]{2,1,0:T(8,128)(2,1)S(1)} %copy-done.2), channel_id=1, source_target_pairs={{0,1},{1,2},{2,3},{3,4},{4,5},{5,6},{6,7},{7,8},{8,9},{9,10},{10,1... | collective-permute-start | bytes 1572872 | tf_op jit(solution)/shard_map/ppermute | solution.py:379
  (12 other events, 167.7 us)

commit v3 on v2

--- a/solution.py
+++ b/solution.py
@@ -428,13 +428,14 @@
     by_x = [all_z] + [shift(all_z, x=s) for s in range(1, X)]
     before, after = halo(packed)
     far = mid_far(info, mid_far_src, mid_far_mat, rings)
-    *by_x, coef, packed, far = tie(*by_x, coef, packed, far)
-    all_x = join(by_x)
-    other = shift(all_x, c=1)
+    coef, packed, far = tie(coef, packed, far)
     coef_before, coef_after = halo(coef)
     near, far_v, tb_v, both = near_field(
         info, near_src.T, near_count, (before, packed, after), near_mat, leaf_far_mat, target_basis, leaf_down
     )
+    by_x[1], near, coef_before, coef_after = tie(by_x[1], near, coef_before, coef_after)
+    all_x = join(by_x)
+    other = shift(all_x, c=1)
     base = leaf_far(info, leaf_far_src.T, (coef_before, coef, coef_after), far_v, tb_v, near)
     top_local = top_far(info, top_far_src, all_x, other, top_far_mat)
     return tail(top_local, far, mid_down, base, both)

time: 110 us -> 99.7 us (0.906)
  waiting for transfers between devices: 21.7 us -> 4.13 us
  starting transfers between devices: 52.6 us -> 61.4 us
    ppermute x4, waiting for transfers between devices: 9.53 us -> 0.01 us  [some(): return lax.ppermute(a, BOTH, pairs)]
    ppermute x21, waiting for transfers between devices: 12.2 us -> 4.12 us  [shift(): return lax.ppermute(a, BOTH, pairs)]
    ppermute x4, starting transfers between devices: 15.6 us -> 23.4 us  [some(): return lax.ppermute(a, BOTH, pairs)]
    unnamed x24 -> x22, local copies, waits for them, and re-layouts: 4.64 us -> 3.85 us
  transfers between devices with their start and end apart: 25 -> 25, of which waited for: 10 -> 6; matrix products, arithmetic and copies ran while one was open for 1% -> 1% of each run, Pallas kernels for 19% -> 21%
where the time goes in v3:
time: 99.7 us; the launch traced here: 99.4 us
  starting transfers between devices  61.4 us (62%)
  Pallas kernels  29.4 us (29%)
  waiting for transfers between devices  4.13 us (4%)
  local copies, waits for them, and re-layouts  3.96 us (4%)
    ppermute x21, starting transfers between devices, shift(): return lax.ppermute(a, BOTH, pairs)  38 us
    ppermute x4, starting transfers between devices, some(): return lax.ppermute(a, BOTH, pairs)  23.4 us
    pallas_call x1, Pallas kernels, near_field(): pl.pallas_call(near_kernel, in_specs=[s] * 3 + [pl.BlockSpec(memory_space...  9.04 us
    pallas_call x1, Pallas kernels, leaf_far(): pl.pallas_call(far_kernel, in_specs=[s] * 2 + [pl.BlockSpec(memory_space=...  6.84 us
    pallas_call x1, Pallas kernels, mid_far(): pl.pallas_call(mid_kernel, in_specs=[s, s] + [pl.BlockSpec(memory_space=p...  5.47 us
    pallas_call x1, Pallas kernels, upsweep(): pl.pallas_call(up_kernel, grid=(4,), in_specs=[leaf, leaf, leaf, pl.Block...  4.83 us
    ppermute x21, waiting for transfers between devices, shift(): return lax.ppermute(a, BOTH, pairs)  4.12 us
    unnamed x22, local copies, waits for them, and re-layouts  3.85 us
  transfers between devices with their start and end apart: 25, of which 6 were waited for; matrix products, arithmetic and copies ran while one was open for 1% of the time, Pallas kernels for 21%

profile of v3, /device:TPU:1, one launch (start us, length us, event | category | flops | bytes accessed | tf_op | source)
XLA Modules:
  0.0 99.4 jit_solution(15456469092119596644)
XLA Ops:
  0.0 4.8 %upsweep.1 = (bf16[32,64,128]{2,1,0:T(8,128)(2,1)}, bf16[32,64,128]{2,1,0:T(8,128)(2,1)}, bf16[288,128]{1,0:T(8,128)(2,1)}) custom-call(bf16[64,64,64]{2,1,0:T(8,128)(2,1)} %c_ref.1, bf16[64,64,64]{2,1,0:T(8,128)(2,1)} %s_ref.1, bf16[64,64,64]{2,1,0:T(8,128)(2,1)} %lu_ref.1, bf16[8,64,64]{2,1,0:T(8,128)(2,1)} %mu_ref.1), custom_call_target="tpu_custom_call" | custom-call | flops 71303168 | bytes 5242880 | tf_op jit(solution)/shard_map/upsweep/pallas_call | solution.py:63
  4.8 2.2 %collective-permute-start = (bf16[288,128]{1,0:T(8,128)(2,1)}, bf16[288,128]{1,0:T(8,128)(2,1)S(1)}, u32[]{:S(2)}, u32[]{:S(2)}) collective-permute-start(bf16[288,128]{1,0:T(8,128)(2,1)} %get-tuple-element.22), channel_id=1, source_target_pairs={{0,1},{1,2},{2,3},{3,0},{4,5},{5,6},{6,7},{7,4},{8,9},{9,10},{10,1... | collective-permute-start | bytes 221192 | tf_op jit(solution)/shard_map/ppermute | solution.py:375
  7.0 2.6 %collective-permute-start.1 = (bf16[288,128]{1,0:T(8,128)(2,1)}, bf16[288,128]{1,0:T(8,128)(2,1)S(1)}, u32[]{:S(2)}, u32[]{:S(2)}) collective-permute-start(bf16[288,128]{1,0:T(8,128)(2,1)} %get-tuple-element.22), channel_id=1, source_target_pairs={{0,2},{1,3},{2,0},{3,1},{4,6},{5,7},{6,4},{7,5},{8,10},{9,11},{10,... | collective-permute-start | bytes 221192 | tf_op jit(solution)/shard_map/ppermute | solution.py:375
  11.7 1.7 %collective-permute-start.3 = (bf16[576,128]{1,0:T(8,128)(2,1)S(1)}, bf16[576,128]{1,0:T(8,128)(2,1)S(1)}, u32[]{:S(2)}, u32[]{:S(2)}) collective-permute-start(bf16[576,128]{1,0:T(8,128)(2,1)S(1)} %constant_dynamic-update-slice_fusion.refs_0_), channel_id=1, source_target_pairs={{0,4},{1,5},{2,6},{3,7},{4,8},{5,9},{6,10},{7,11},{8,12},{9,13},{1... | collective-permute-start | bytes 442376 | tf_op jit(solution)/shard_map/ppermute | solution.py:375
  13.4 5.7 %collective-permute-start.10 = (bf16[576,128]{1,0:T(8,128)(2,1)S(1)}, bf16[576,128]{1,0:T(8,128)(2,1)S(1)}, u32[]{:S(2)}, u32[]{:S(2)}) collective-permute-start(bf16[576,128]{1,0:T(8,128)(2,1)S(1)} %constant_dynamic-update-slice_fusion.2.refs_1_), channel_id=1, source_target_pairs={{0,28},{1,29},{2,30},{3,31},{4,0},{5,1},{6,2},{7,3},{8,4},{9,5},{1... | collective-permute-start | bytes 442376 | tf_op jit(solution)/shard_map/ppermute | solution.py:375
  19.1 2.7 %collective-permute-start.14 = (bf16[576,128]{1,0:T(8,128)(2,1)S(1)}, bf16[576,128]{1,0:T(8,128)(2,1)S(1)}, u32[]{:S(2)}, u32[]{:S(2)}) collective-permute-start(bf16[576,128]{1,0:T(8,128)(2,1)S(1)} %constant_dynamic-update-slice_fusion.refs_0_), channel_id=1, source_target_pairs={{0,28},{1,29},{2,30},{3,31},{4,0},{5,1},{6,2},{7,3},{8,4},{9,5},{1... | collective-permute-start | bytes 442376 | tf_op jit(solution)/shard_map/ppermute | solution.py:375
  21.8 2.7 %collective-permute-start.11 = (bf16[576,128]{1,0:T(8,128)(2,1)S(1)}, bf16[576,128]{1,0:T(8,128)(2,1)S(1)}, u32[]{:S(2)}, u32[]{:S(2)}) collective-permute-start(bf16[576,128]{1,0:T(8,128)(2,1)S(1)} %collective-permute-done.10.refs_15_), channel_id=1, source_target_pairs={{0,28},{1,29},{2,30},{3,31},{4,0},{5,1},{6,2},{7,3},{8,4},{9,5},{1... | collective-permute-start | bytes 442376 | tf_op jit(solution)/shard_map/ppermute | solution.py:375
  25.3 3.2 %collective-permute-start.15 = (bf16[576,128]{1,0:T(8,128)(2,1)S(1)}, bf16[576,128]{1,0:T(8,128)(2,1)S(1)}, u32[]{:S(2)}, u32[]{:S(2)}) collective-permute-start(bf16[576,128]{1,0:T(8,128)(2,1)S(1)} %collective-permute-done.14.refs_14_), channel_id=1, source_target_pairs={{0,28},{1,29},{2,30},{3,31},{4,0},{5,1},{6,2},{7,3},{8,4},{9,5},{1... | collective-permute-start | bytes 442376 | tf_op jit(solution)/shard_map/ppermute | solution.py:375
  28.8 2.9 %collective-permute-start.12 = (bf16[576,128]{1,0:T(8,128)(2,1)S(1)}, bf16[576,128]{1,0:T(8,128)(2,1)S(1)}, u32[]{:S(2)}, u32[]{:S(2)}) collective-permute-start(bf16[576,128]{1,0:T(8,128)(2,1)S(1)} %collective-permute-done.11.refs_13_), channel_id=1, source_target_pairs={{0,28},{1,29},{2,30},{3,31},{4,0},{5,1},{6,2},{7,3},{8,4},{9,5},{1... | collective-permute-start | bytes 442376 | tf_op jit(solution)/shard_map/ppermute | solution.py:375
  31.8 2.9 %collective-permute-start.16 = (bf16[576,128]{1,0:T(8,128)(2,1)S(1)}, bf16[576,128]{1,0:T(8,128)(2,1)S(1)}, u32[]{:S(2)}, u32[]{:S(2)}) collective-permute-start(bf16[576,128]{1,0:T(8,128)(2,1)S(1)} %collective-permute-done.15.refs_12_), channel_id=1, source_target_pairs={{0,28},{1,29},{2,30},{3,31},{4,0},{5,1},{6,2},{7,3},{8,4},{9,5},{1... | collective-permute-start | bytes 442376 | tf_op jit(solution)/shard_map/ppermute | solution.py:375
  34.9 2.8 %collective-permute-start.13 = (bf16[576,128]{1,0:T(8,128)(2,1)S(1)}, bf16[576,128]{1,0:T(8,128)(2,1)S(1)}, u32[]{:S(2)}, u32[]{:S(2)}) collective-permute-start(bf16[576,128]{1,0:T(8,128)(2,1)S(1)} %collective-permute-done.12.refs_11_), channel_id=1, source_target_pairs={{0,28},{1,29},{2,30},{3,31},{4,0},{5,1},{6,2},{7,3},{8,4},{9,5},{1... | collective-permute-start | bytes 442376 | tf_op jit(solution)/shard_map/ppermute | solution.py:375
  37.9 2.4 %collective-permute-done.9.refs_8_ = bf16[576,128]{1,0:T(8,128)(2,1)S(1)} collective-permute-done((bf16[576,128]{1,0:T(8,128)(2,1)S(1)}, bf16[576,128]{1,0:T(8,128)(2,1)S(1)}, u32[]{:S(2)}, u32[]{:S(2)}) %collective-permute-start.9) | collective-permute-done | bytes 147488 | tf_op jit(solution)/shard_map/ppermute | solution.py:375
  41.0 2.0 %collective-permute-start.18 = (bf16[32,64,128]{2,1,0:T(8,128)(2,1)}, bf16[32,64,128]{2,1,0:T(8,128)(2,1)S(1)}, u32[]{:S(2)}, u32[]{:S(2)}) collective-permute-start(bf16[32,64,128]{2,1,0:T(8,128)(2,1)} %get-tuple-element.28.co), channel_id=1, source_target_pairs={{0,1},{1,2},{2,3},{3,4},{4,5},{5,6},{6,7},{7,8},{8,9},{9,10},{10,1... | collective-permute-start | bytes 1572872 | tf_op jit(solution)/shard_map/ppermute | solution.py:379
  43.0 12.5 %collective-permute-start.19 = (bf16[32,64,128]{2,1,0:T(8,128)(2,1)}, bf16[32,64,128]{2,1,0:T(8,128)(2,1)}, u32[]{:S(2)}, u32[]{:S(2)}) collective-permute-start(bf16[32,64,128]{2,1,0:T(8,128)(2,1)} %get-tuple-element.28.co), channel_id=1, source_target_pairs={{1,0},{2,1},{3,2},{4,3},{5,4},{6,5},{7,6},{8,7},{9,8},{10,9},{11,1... | collective-permute-start | bytes 1572872 | tf_op jit(solution)/shard_map/ppermute | solution.py:379
  55.7 1.6 %copy-done = bf16[8,16,64,64]{3,2,1,0:T(8,128)(2,1)S(1)} copy-done((bf16[8,16,64,64]{3,2,1,0:T(8,128)(2,1)S(1)}, bf16[8,16,64,64]{3,2,1,0:T(8,128)(2,1)}, u32[]{:S(2)}) %copy-start) | copy-done | bytes 1048600
  58.0 5.5 %mid_far.1.far = f32[8,64,64]{2,1,0:T(8,128)S(1)} custom-call(s32[6]{0:T(128)S(1)} %stack.27.info, s32[8,16]{1,0:T(8,128)S(1)} %copy-done.7, bf16[8,16,64,64]{3,2,1,0:T(8,128)(2,1)S(1)} %copy-done, bf16[576,128]{1,0:T(8,128)(2,1)S(1)} %constant_dynamic-update-slice_fusion.refs_0_, bf16[576,128]{1,0:T(8,128)(2,1)S(1)} %constant_dynamic-update-slice_fusion.2.refs_1_, ...), custom_call_target="tpu_custom_call" | custom-call | flops 67108864 | bytes 6291456 | tf_op jit(solution)/shard_map/mid_far/pallas_call | solution.py:320
  63.5 1.9 %collective-permute-start.20 = (bf16[32,64,128]{2,1,0:T(8,128)(2,1)}, bf16[32,64,128]{2,1,0:T(8,128)(2,1)S(1)}, u32[]{:S(2)}, u32[]{:S(2)}) collective-permute-start(bf16[32,64,128]{2,1,0:T(8,128)(2,1)} %get-tuple-element.30.ko), channel_id=1, source_target_pairs={{0,1},{1,2},{2,3},{3,4},{4,5},{5,6},{6,7},{7,8},{8,9},{9,10},{10,1... | collective-permute-start | bytes 1572872 | tf_op jit(solution)/shard_map/ppermute | solution.py:379
  65.4 7.0 %collective-permute-start.21 = (bf16[32,64,128]{2,1,0:T(8,128)(2,1)}, bf16[32,64,128]{2,1,0:T(8,128)(2,1)S(1)}, u32[]{:S(2)}, u32[]{:S(2)}) collective-permute-start(bf16[32,64,128]{2,1,0:T(8,128)(2,1)} %get-tuple-element.30.ko), channel_id=1, source_target_pairs={{1,0},{2,1},{3,2},{4,3},{5,4},{6,5},{7,6},{8,7},{9,8},{10,9},{11,1... | collective-permute-start | bytes 1572872 | tf_op jit(solution)/shard_map/ppermute | solution.py:379
  72.4 1.3 %collective-permute-start.17 = (bf16[1024,128]{1,0:T(8,128)(2,1)S(1)}, bf16[1024,128]{1,0:T(8,128)(2,1)S(1)}, u32[]{:S(2)}, u32[]{:S(2)}) collective-permute-start(bf16[1024,128]{1,0:T(8,128)(2,1)S(1)} %pick_tops.1.a), channel_id=1, source_target_pairs={{0,64},{1,65},{2,66},{3,67},{4,68},{5,69},{6,70},{7,71},{8,72},{9,... | collective-permute-start | bytes 786440 | tf_op jit(solution)/shard_map/ppermute | solution.py:375
  73.6 2.5 %collective-permute-start.22 = (bf16[1024,128]{1,0:T(8,128)(2,1)S(1)}, bf16[1024,128]{1,0:T(8,128)(2,1)S(1)}, u32[]{:S(2)}, u32[]{:S(2)}) collective-permute-start(bf16[1024,128]{1,0:T(8,128)(2,1)S(1)} %pick_tops.1.a), channel_id=1, source_target_pairs={{0,128},{1,129},{2,130},{3,131},{4,132},{5,133},{6,134},{7,135},{8... | collective-permute-start | bytes 786440 | tf_op jit(solution)/shard_map/ppermute | solution.py:375
  77.3 9.0 %near.1 = (f32[64,64,64]{2,1,0:T(8,128)S(1)}, bf16[64,8,64,64]{3,2,1,0:T(8,128)(2,1)S(1)}, bf16[64,64,64]{2,1,0:T(8,128)(2,1)S(1)}, bf16[64,64,64]{2,1,0:T(8,128)(2,1)S(1)}) custom-call(s32[6]{0:T(128)} %copy-done.4, s32[8,64]{1,0:T(8,128)} %bitcast.9, s32[64]{0:T(128)} %cnt.1, bf16[32,64,128]{2,1,0:T(8,128)(2,1)} %copy-done.9, ...), custom_call_target="tpu_custom_call" | custom-call | flops 301989888 | bytes 25165824 | tf_op jit(solution)/shard_map/near/pallas_call | solution.py:149
  86.5 2.7 %collective-permute-start.24 = (bf16[4096,128]{1,0:T(8,128)(2,1)S(1)}, bf16[4096,128]{1,0:T(8,128)(2,1)S(1)}, u32[]{:S(2)}, u32[]{:S(2)}) collective-permute-start(bf16[4096,128]{1,0:T(8,128)(2,1)S(1)} %join.1.own), channel_id=1, source_target_pairs={{0,32},{1,33},{2,34},{3,35},{4,36},{5,37},{6,38},{7,39},{8,40},{9,... | collective-permute-start | bytes 3145736 | tf_op jit(solution)/shard_map/ppermute | solution.py:375
  89.9 6.8 %leaf_far.1.base = f32[64,64,64]{2,1,0:T(8,128)S(1)} custom-call(s32[6]{0:T(128)S(1)} %copy-done.5, s32[8,64]{1,0:T(8,128)S(1)} %bitcast.8, bf16[32,64,128]{2,1,0:T(8,128)(2,1)S(1)} %collective-permute-done.20.ku, bf16[32,64,128]{2,1,0:T(8,128)(2,1)S(1)} %copy-done.2, bf16[32,64,128]{2,1,0:T(8,128)(2,1)S(1)} %collective-permute-done.21.kd, ...), custom_call_target="tpu_custom_call" | custom-call | flops 301989888 | bytes 16777216 | tf_op jit(solution)/shard_map/leaf_far/pallas_call | solution.py:201
  97.8 1.4 %tail.1 = bf16[64,64,64]{2,1,0:T(8,128)(2,1)} custom-call(bf16[64,64]{1,0:T(8,128)(2,1)S(1)} %top_far.1.top_ref, f32[8,64,64]{2,1,0:T(8,128)S(1)} %mid_far.1.far, bf16[8,64,64]{2,1,0:T(8,128)(2,1)S(1)} %copy-done.3, f32[64,64,64]{2,1,0:T(8,128)S(1)} %leaf_far.1.base, bf16[64,64,64]{2,1,0:T(8,128)(2,1)S(1)} %get-tuple-element.38.both), custom_call_target="tpu_custom_call" | custom-call | flops 37748736 | bytes 6291456 | tf_op jit(solution)/shard_map/tail/pallas_call | solution.py:350
  (59 shorter events, 8.2 us)
Async XLA Ops:
  4.8 6.8 %collective-permute-start = (bf16[288,128]{1,0:T(8,128)(2,1)}, bf16[288,128]{1,0:T(8,128)(2,1)S(1)}, u32[]{:S(2)}, u32[]{:S(2)}) collective-permute-start(bf16[288,128]{1,0:T(8,128)(2,1)} %get-tuple-element.22), channel_id=1, source_target_pairs={{0,1},{1,2},{2,3},{3,0},{4,5},{5,6},{6,7},{7,4},{8,9},{9,10},{10,1... | collective-permute-start | bytes 221192 | tf_op jit(solution)/shard_map/ppermute | solution.py:375
  7.0 6.3 %collective-permute-start.1 = (bf16[288,128]{1,0:T(8,128)(2,1)}, bf16[288,128]{1,0:T(8,128)(2,1)S(1)}, u32[]{:S(2)}, u32[]{:S(2)}) collective-permute-start(bf16[288,128]{1,0:T(8,128)(2,1)} %get-tuple-element.22), channel_id=1, source_target_pairs={{0,2},{1,3},{2,0},{3,1},{4,6},{5,7},{6,4},{7,5},{8,10},{9,11},{10,... | collective-permute-start | bytes 221192 | tf_op jit(solution)/shard_map/ppermute | solution.py:375
  11.7 10.1 %collective-permute-start.3 = (bf16[576,128]{1,0:T(8,128)(2,1)S(1)}, bf16[576,128]{1,0:T(8,128)(2,1)S(1)}, u32[]{:S(2)}, u32[]{:S(2)}) collective-permute-start(bf16[576,128]{1,0:T(8,128)(2,1)S(1)} %constant_dynamic-update-slice_fusion.refs_0_), channel_id=1, source_target_pairs={{0,4},{1,5},{2,6},{3,7},{4,8},{5,9},{6,10},{7,11},{8,12},{9,13},{1... | collective-permute-start | bytes 442376 | tf_op jit(solution)/shard_map/ppermute | solution.py:375
  13.4 8.4 %collective-permute-start.10 = (bf16[576,128]{1,0:T(8,128)(2,1)S(1)}, bf16[576,128]{1,0:T(8,128)(2,1)S(1)}, u32[]{:S(2)}, u32[]{:S(2)}) collective-permute-start(bf16[576,128]{1,0:T(8,128)(2,1)S(1)} %constant_dynamic-update-slice_fusion.2.refs_1_), channel_id=1, source_target_pairs={{0,28},{1,29},{2,30},{3,31},{4,0},{5,1},{6,2},{7,3},{8,4},{9,5},{1... | collective-permute-start | bytes 442376 | tf_op jit(solution)/shard_map/ppermute | solution.py:375
  19.1 5.4 %collective-permute-start.4 = (bf16[576,128]{1,0:T(8,128)(2,1)S(1)}, bf16[576,128]{1,0:T(8,128)(2,1)S(1)}, u32[]{:S(2)}, u32[]{:S(2)}) collective-permute-start(bf16[576,128]{1,0:T(8,128)(2,1)S(1)} %constant_dynamic-update-slice_fusion.2.refs_1_), channel_id=1, source_target_pairs={{0,4},{1,5},{2,6},{3,7},{4,8},{5,9},{6,10},{7,11},{8,12},{9,13},{1... | collective-permute-start | bytes 442376 | tf_op jit(solution)/shard_map/ppermute | solution.py:375
  19.1 6.1 %collective-permute-start.14 = (bf16[576,128]{1,0:T(8,128)(2,1)S(1)}, bf16[576,128]{1,0:T(8,128)(2,1)S(1)}, u32[]{:S(2)}, u32[]{:S(2)}) collective-permute-start(bf16[576,128]{1,0:T(8,128)(2,1)S(1)} %constant_dynamic-update-slice_fusion.refs_0_), channel_id=1, source_target_pairs={{0,28},{1,29},{2,30},{3,31},{4,0},{5,1},{6,2},{7,3},{8,4},{9,5},{1... | collective-permute-start | bytes 442376 | tf_op jit(solution)/shard_map/ppermute | solution.py:375
  21.8 7.0 %collective-permute-start.5 = (bf16[576,128]{1,0:T(8,128)(2,1)S(1)}, bf16[576,128]{1,0:T(8,128)(2,1)S(1)}, u32[]{:S(2)}, u32[]{:S(2)}) collective-permute-start(bf16[576,128]{1,0:T(8,128)(2,1)S(1)} %collective-permute-done.3.refs_2_), channel_id=1, source_target_pairs={{0,4},{1,5},{2,6},{3,7},{4,8},{5,9},{6,10},{7,11},{8,12},{9,13},{1... | collective-permute-start | bytes 442376 | tf_op jit(solution)/shard_map/ppermute | solution.py:375
  21.8 7.0 %collective-permute-start.11 = (bf16[576,128]{1,0:T(8,128)(2,1)S(1)}, bf16[576,128]{1,0:T(8,128)(2,1)S(1)}, u32[]{:S(2)}, u32[]{:S(2)}) collective-permute-start(bf16[576,128]{1,0:T(8,128)(2,1)S(1)} %collective-permute-done.10.refs_15_), channel_id=1, source_target_pairs={{0,28},{1,29},{2,30},{3,31},{4,0},{5,1},{6,2},{7,3},{8,4},{9,5},{1... | collective-permute-start | bytes 442376 | tf_op jit(solution)/shard_map/ppermute | solution.py:375
  24.5 7.3 %collective-permute-start.6 = (bf16[576,128]{1,0:T(8,128)(2,1)S(1)}, bf16[576,128]{1,0:T(8,128)(2,1)S(1)}, u32[]{:S(2)}, u32[]{:S(2)}) collective-permute-start(bf16[576,128]{1,0:T(8,128)(2,1)S(1)} %collective-permute-done.4.refs_3_), channel_id=1, source_target_pairs={{0,4},{1,5},{2,6},{3,7},{4,8},{5,9},{6,10},{7,11},{8,12},{9,13},{1... | collective-permute-start | bytes 442376 | tf_op jit(solution)/shard_map/ppermute | solution.py:375
  25.3 6.6 %collective-permute-start.15 = (bf16[576,128]{1,0:T(8,128)(2,1)S(1)}, bf16[576,128]{1,0:T(8,128)(2,1)S(1)}, u32[]{:S(2)}, u32[]{:S(2)}) collective-permute-start(bf16[576,128]{1,0:T(8,128)(2,1)S(1)} %collective-permute-done.14.refs_14_), channel_id=1, source_target_pairs={{0,28},{1,29},{2,30},{3,31},{4,0},{5,1},{6,2},{7,3},{8,4},{9,5},{1... | collective-permute-start | bytes 442376 | tf_op jit(solution)/shard_map/ppermute | solution.py:375
  28.8 6.1 %collective-permute-start.7 = (bf16[576,128]{1,0:T(8,128)(2,1)S(1)}, bf16[576,128]{1,0:T(8,128)(2,1)S(1)}, u32[]{:S(2)}, u32[]{:S(2)}) collective-permute-start(bf16[576,128]{1,0:T(8,128)(2,1)S(1)} %collective-permute-done.5.refs_4_), channel_id=1, source_target_pairs={{0,4},{1,5},{2,6},{3,7},{4,8},{5,9},{6,10},{7,11},{8,12},{9,13},{1... | collective-permute-start | bytes 442376 | tf_op jit(solution)/shard_map/ppermute | solution.py:375
  28.8 6.1 %collective-permute-start.12 = (bf16[576,128]{1,0:T(8,128)(2,1)S(1)}, bf16[576,128]{1,0:T(8,128)(2,1)S(1)}, u32[]{:S(2)}, u32[]{:S(2)}) collective-permute-start(bf16[576,128]{1,0:T(8,128)(2,1)S(1)} %collective-permute-done.11.refs_13_), channel_id=1, source_target_pairs={{0,28},{1,29},{2,30},{3,31},{4,0},{5,1},{6,2},{7,3},{8,4},{9,5},{1... | collective-permute-start | bytes 442376 | tf_op jit(solution)/shard_map/ppermute | solution.py:375
  31.8 6.1 %collective-permute-start.8 = (bf16[576,128]{1,0:T(8,128)(2,1)S(1)}, bf16[576,128]{1,0:T(8,128)(2,1)S(1)}, u32[]{:S(2)}, u32[]{:S(2)}) collective-permute-start(bf16[576,128]{1,0:T(8,128)(2,1)S(1)} %collective-permute-done.6.refs_5_), channel_id=1, source_target_pairs={{0,4},{1,5},{2,6},{3,7},{4,8},{5,9},{6,10},{7,11},{8,12},{9,13},{1... | collective-permute-start | bytes 442376 | tf_op jit(solution)/shard_map/ppermute | solution.py:375
  31.8 6.1 %collective-permute-start.16 = (bf16[576,128]{1,0:T(8,128)(2,1)S(1)}, bf16[576,128]{1,0:T(8,128)(2,1)S(1)}, u32[]{:S(2)}, u32[]{:S(2)}) collective-permute-start(bf16[576,128]{1,0:T(8,128)(2,1)S(1)} %collective-permute-done.15.refs_12_), channel_id=1, source_target_pairs={{0,28},{1,29},{2,30},{3,31},{4,0},{5,1},{6,2},{7,3},{8,4},{9,5},{1... | collective-permute-start | bytes 442376 | tf_op jit(solution)/shard_map/ppermute | solution.py:375
  34.9 5.4 %collective-permute-start.9 = (bf16[576,128]{1,0:T(8,128)(2,1)S(1)}, bf16[576,128]{1,0:T(8,128)(2,1)S(1)}, u32[]{:S(2)}, u32[]{:S(2)}) collective-permute-start(bf16[576,128]{1,0:T(8,128)(2,1)S(1)} %collective-permute-done.7.refs_6_), channel_id=1, source_target_pairs={{0,4},{1,5},{2,6},{3,7},{4,8},{5,9},{6,10},{7,11},{8,12},{9,13},{1... | collective-permute-start | bytes 442376 | tf_op jit(solution)/shard_map/ppermute | solution.py:375
  34.9 5.4 %collective-permute-start.13 = (bf16[576,128]{1,0:T(8,128)(2,1)S(1)}, bf16[576,128]{1,0:T(8,128)(2,1)S(1)}, u32[]{:S(2)}, u32[]{:S(2)}) collective-permute-start(bf16[576,128]{1,0:T(8,128)(2,1)S(1)} %collective-permute-done.12.refs_11_), channel_id=1, source_target_pairs={{0,28},{1,29},{2,30},{3,31},{4,0},{5,1},{6,2},{7,3},{8,4},{9,5},{1... | collective-permute-start | bytes 442376 | tf_op jit(solution)/shard_map/ppermute | solution.py:375
  41.0 32.6 %collective-permute-start.18 = (bf16[32,64,128]{2,1,0:T(8,128)(2,1)}, bf16[32,64,128]{2,1,0:T(8,128)(2,1)S(1)}, u32[]{:S(2)}, u32[]{:S(2)}) collective-permute-start(bf16[32,64,128]{2,1,0:T(8,128)(2,1)} %get-tuple-element.28.co), channel_id=1, source_target_pairs={{0,1},{1,2},{2,3},{3,4},{4,5},{5,6},{6,7},{7,8},{8,9},{9,10},{10,1... | collective-permute-start | bytes 1572872 | tf_op jit(solution)/shard_map/ppermute | solution.py:379
  43.0 33.1 %collective-permute-start.19 = (bf16[32,64,128]{2,1,0:T(8,128)(2,1)}, bf16[32,64,128]{2,1,0:T(8,128)(2,1)}, u32[]{:S(2)}, u32[]{:S(2)}) collective-permute-start(bf16[32,64,128]{2,1,0:T(8,128)(2,1)} %get-tuple-element.28.co), channel_id=1, source_target_pairs={{1,0},{2,1},{3,2},{4,3},{5,4},{6,5},{7,6},{8,7},{9,8},{10,9},{11,1... | collective-permute-start | bytes 1572872 | tf_op jit(solution)/shard_map/ppermute | solution.py:379
  63.5 22.9 %collective-permute-start.20 = (bf16[32,64,128]{2,1,0:T(8,128)(2,1)}, bf16[32,64,128]{2,1,0:T(8,128)(2,1)S(1)}, u32[]{:S(2)}, u32[]{:S(2)}) collective-permute-start(bf16[32,64,128]{2,1,0:T(8,128)(2,1)} %get-tuple-element.30.ko), channel_id=1, source_target_pairs={{0,1},{1,2},{2,3},{3,4},{4,5},{5,6},{6,7},{7,8},{8,9},{9,10},{10,1... | collective-permute-start | bytes 1572872 | tf_op jit(solution)/shard_map/ppermute | solution.py:379
  65.4 21.0 %collective-permute-start.21 = (bf16[32,64,128]{2,1,0:T(8,128)(2,1)}, bf16[32,64,128]{2,1,0:T(8,128)(2,1)S(1)}, u32[]{:S(2)}, u32[]{:S(2)}) collective-permute-start(bf16[32,64,128]{2,1,0:T(8,128)(2,1)} %get-tuple-element.30.ko), channel_id=1, source_target_pairs={{1,0},{2,1},{3,2},{4,3},{5,4},{6,5},{7,6},{8,7},{9,8},{10,9},{11,1... | collective-permute-start | bytes 1572872 | tf_op jit(solution)/shard_map/ppermute | solution.py:379
  72.4 14.0 %collective-permute-start.17 = (bf16[1024,128]{1,0:T(8,128)(2,1)S(1)}, bf16[1024,128]{1,0:T(8,128)(2,1)S(1)}, u32[]{:S(2)}, u32[]{:S(2)}) collective-permute-start(bf16[1024,128]{1,0:T(8,128)(2,1)S(1)} %pick_tops.1.a), channel_id=1, source_target_pairs={{0,64},{1,65},{2,66},{3,67},{4,68},{5,69},{6,70},{7,71},{8,72},{9,... | collective-permute-start | bytes 786440 | tf_op jit(solution)/shard_map/ppermute | solution.py:375
  73.6 12.8 %collective-permute-start.22 = (bf16[1024,128]{1,0:T(8,128)(2,1)S(1)}, bf16[1024,128]{1,0:T(8,128)(2,1)S(1)}, u32[]{:S(2)}, u32[]{:S(2)}) collective-permute-start(bf16[1024,128]{1,0:T(8,128)(2,1)S(1)} %pick_tops.1.a), channel_id=1, source_target_pairs={{0,128},{1,129},{2,130},{3,131},{4,132},{5,133},{6,134},{7,135},{8... | collective-permute-start | bytes 786440 | tf_op jit(solution)/shard_map/ppermute | solution.py:375
  76.1 10.3 %collective-permute-start.23 = (bf16[1024,128]{1,0:T(8,128)(2,1)S(1)}, bf16[1024,128]{1,0:T(8,128)(2,1)S(1)}, u32[]{:S(2)}, u32[]{:S(2)}) collective-permute-start(bf16[1024,128]{1,0:T(8,128)(2,1)S(1)} %pick_tops.1.a), channel_id=1, source_target_pairs={{0,192},{1,193},{2,194},{3,195},{4,196},{5,197},{6,198},{7,199},{8... | collective-permute-start | bytes 786440 | tf_op jit(solution)/shard_map/ppermute | solution.py:375
  86.5 10.2 %collective-permute-start.24 = (bf16[4096,128]{1,0:T(8,128)(2,1)S(1)}, bf16[4096,128]{1,0:T(8,128)(2,1)S(1)}, u32[]{:S(2)}, u32[]{:S(2)}) collective-permute-start(bf16[4096,128]{1,0:T(8,128)(2,1)S(1)} %join.1.own), channel_id=1, source_target_pairs={{0,32},{1,33},{2,34},{3,35},{4,36},{5,37},{6,38},{7,39},{8,40},{9,... | collective-permute-start | bytes 3145736 | tf_op jit(solution)/shard_map/ppermute | solution.py:375
  (11 other events, 82.2 us)

commit v4 on v3

--- a/solution.py
+++ b/solution.py
@@ -424,11 +424,11 @@
     rings = [rings[s, h] for s in range(8) for h in range(2)]
 
     all_z = pick_tops(rings)
-    all_z, rings[0], packed = tie(all_z, rings[0], packed)
+    all_z, rings[0], packed, coef = tie(all_z, rings[0], packed, coef)
     by_x = [all_z] + [shift(all_z, x=s) for s in range(1, X)]
     before, after = halo(packed)
     far = mid_far(info, mid_far_src, mid_far_mat, rings)
-    coef, packed, far = tie(coef, packed, far)
+    packed, far = tie(packed, far)
     coef_before, coef_after = halo(coef)
     near, far_v, tb_v, both = near_field(
         info, near_src.T, near_count, (before, packed, after), near_mat, leaf_far_mat, target_basis, leaf_down

time: 99.7 us -> 103 us (1.033)
  Pallas kernels: 29.4 us -> 31.4 us
    unnamed x22 -> x24, local copies, waits for them, and re-layouts: 3.85 us -> 4.71 us
  transfers between devices with their start and end apart: 25 -> 25, of which waited for: 6 -> 7; matrix products, arithmetic and copies ran while one was open for 1% -> 1% of each run, Pallas kernels for 21% -> 22%
where the time goes in v4:
time: 103 us
  starting transfers between devices  61.8 us (60%)
  Pallas kernels  31.4 us (30%)
  local copies, waits for them, and re-layouts  4.82 us (5%)
  waiting for transfers between devices  4.45 us (4%)
    ppermute x21, starting transfers between devices, shift(): return lax.ppermute(a, BOTH, pairs)  38.4 us
    ppermute x4, starting transfers between devices, some(): return lax.ppermute(a, BOTH, pairs)  23.4 us
    pallas_call x1, Pallas kernels, near_field(): pl.pallas_call(near_kernel, in_specs=[s] * 3 + [pl.BlockSpec(memory_space...  9.03 us
    pallas_call x1, Pallas kernels, leaf_far(): pl.pallas_call(far_kernel, in_specs=[s] * 2 + [pl.BlockSpec(memory_space=...  7.83 us
    pallas_call x1, Pallas kernels, mid_far(): pl.pallas_call(mid_kernel, in_specs=[s, s] + [pl.BlockSpec(memory_space=p...  5.47 us
    pallas_call x1, Pallas kernels, upsweep(): pl.pallas_call(up_kernel, grid=(4,), in_specs=[leaf, leaf, leaf, pl.Block...  4.83 us
    unnamed x24, local copies, waits for them, and re-layouts  4.71 us
    ppermute x21, waiting for transfers between devices, shift(): return lax.ppermute(a, BOTH, pairs)  4.09 us
  transfers between devices with their start and end apart: 25, of which 7 were waited for; matrix products, arithmetic and copies ran while one was open for 1% of the time, Pallas kernels for 22%

profile of v4, /device:TPU:1, one launch (start us, length us, event | category | flops | bytes accessed | tf_op | source)
XLA Modules:
  0.0 102.9 jit_solution(10937441506044965296)
XLA Ops:
  0.0 4.8 %upsweep.1 = (bf16[32,64,128]{2,1,0:T(8,128)(2,1)}, bf16[32,64,128]{2,1,0:T(8,128)(2,1)}, bf16[288,128]{1,0:T(8,128)(2,1)}) custom-call(bf16[64,64,64]{2,1,0:T(8,128)(2,1)} %c_ref.1, bf16[64,64,64]{2,1,0:T(8,128)(2,1)} %s_ref.1, bf16[64,64,64]{2,1,0:T(8,128)(2,1)} %lu_ref.1, bf16[8,64,64]{2,1,0:T(8,128)(2,1)} %mu_ref.1), custom_call_target="tpu_custom_call" | custom-call | flops 71303168 | bytes 5242880 | tf_op jit(solution)/shard_map/upsweep/pallas_call | solution.py:63
  4.8 2.2 %collective-permute-start = (bf16[288,128]{1,0:T(8,128)(2,1)}, bf16[288,128]{1,0:T(8,128)(2,1)S(1)}, u32[]{:S(2)}, u32[]{:S(2)}) collective-permute-start(bf16[288,128]{1,0:T(8,128)(2,1)} %get-tuple-element.22), channel_id=1, source_target_pairs={{0,1},{1,2},{2,3},{3,0},{4,5},{5,6},{6,7},{7,4},{8,9},{9,10},{10,1... | collective-permute-start | bytes 221192 | tf_op jit(solution)/shard_map/ppermute | solution.py:375
  7.0 2.6 %collective-permute-start.1 = (bf16[288,128]{1,0:T(8,128)(2,1)}, bf16[288,128]{1,0:T(8,128)(2,1)S(1)}, u32[]{:S(2)}, u32[]{:S(2)}) collective-permute-start(bf16[288,128]{1,0:T(8,128)(2,1)} %get-tuple-element.22), channel_id=1, source_target_pairs={{0,2},{1,3},{2,0},{3,1},{4,6},{5,7},{6,4},{7,5},{8,10},{9,11},{10,... | collective-permute-start | bytes 221192 | tf_op jit(solution)/shard_map/ppermute | solution.py:375
  11.7 1.7 %collective-permute-start.3 = (bf16[576,128]{1,0:T(8,128)(2,1)S(1)}, bf16[576,128]{1,0:T(8,128)(2,1)S(1)}, u32[]{:S(2)}, u32[]{:S(2)}) collective-permute-start(bf16[576,128]{1,0:T(8,128)(2,1)S(1)} %constant_dynamic-update-slice_fusion.refs_0_), channel_id=1, source_target_pairs={{0,4},{1,5},{2,6},{3,7},{4,8},{5,9},{6,10},{7,11},{8,12},{9,13},{1... | collective-permute-start | bytes 442376 | tf_op jit(solution)/shard_map/ppermute | solution.py:375
  13.4 5.7 %collective-permute-start.10 = (bf16[576,128]{1,0:T(8,128)(2,1)S(1)}, bf16[576,128]{1,0:T(8,128)(2,1)S(1)}, u32[]{:S(2)}, u32[]{:S(2)}) collective-permute-start(bf16[576,128]{1,0:T(8,128)(2,1)S(1)} %constant_dynamic-update-slice_fusion.2.refs_1_), channel_id=1, source_target_pairs={{0,28},{1,29},{2,30},{3,31},{4,0},{5,1},{6,2},{7,3},{8,4},{9,5},{1... | collective-permute-start | bytes 442376 | tf_op jit(solution)/shard_map/ppermute | solution.py:375
  19.1 2.7 %collective-permute-start.14 = (bf16[576,128]{1,0:T(8,128)(2,1)S(1)}, bf16[576,128]{1,0:T(8,128)(2,1)S(1)}, u32[]{:S(2)}, u32[]{:S(2)}) collective-permute-start(bf16[576,128]{1,0:T(8,128)(2,1)S(1)} %constant_dynamic-update-slice_fusion.refs_0_), channel_id=1, source_target_pairs={{0,28},{1,29},{2,30},{3,31},{4,0},{5,1},{6,2},{7,3},{8,4},{9,5},{1... | collective-permute-start | bytes 442376 | tf_op jit(solution)/shard_map/ppermute | solution.py:375
  21.8 2.7 %collective-permute-start.11 = (bf16[576,128]{1,0:T(8,128)(2,1)S(1)}, bf16[576,128]{1,0:T(8,128)(2,1)S(1)}, u32[]{:S(2)}, u32[]{:S(2)}) collective-permute-start(bf16[576,128]{1,0:T(8,128)(2,1)S(1)} %collective-permute-done.10.refs_15_), channel_id=1, source_target_pairs={{0,28},{1,29},{2,30},{3,31},{4,0},{5,1},{6,2},{7,3},{8,4},{9,5},{1... | collective-permute-start | bytes 442376 | tf_op jit(solution)/shard_map/ppermute | solution.py:375
  25.3 3.2 %collective-permute-start.15 = (bf16[576,128]{1,0:T(8,128)(2,1)S(1)}, bf16[576,128]{1,0:T(8,128)(2,1)S(1)}, u32[]{:S(2)}, u32[]{:S(2)}) collective-permute-start(bf16[576,128]{1,0:T(8,128)(2,1)S(1)} %collective-permute-done.14.refs_14_), channel_id=1, source_target_pairs={{0,28},{1,29},{2,30},{3,31},{4,0},{5,1},{6,2},{7,3},{8,4},{9,5},{1... | collective-permute-start | bytes 442376 | tf_op jit(solution)/shard_map/ppermute | solution.py:375
  28.8 2.9 %collective-permute-start.12 = (bf16[576,128]{1,0:T(8,128)(2,1)S(1)}, bf16[576,128]{1,0:T(8,128)(2,1)S(1)}, u32[]{:S(2)}, u32[]{:S(2)}) collective-permute-start(bf16[576,128]{1,0:T(8,128)(2,1)S(1)} %collective-permute-done.11.refs_13_), channel_id=1, source_target_pairs={{0,28},{1,29},{2,30},{3,31},{4,0},{5,1},{6,2},{7,3},{8,4},{9,5},{1... | collective-permute-start | bytes 442376 | tf_op jit(solution)/shard_map/ppermute | solution.py:375
  31.8 2.9 %collective-permute-start.16 = (bf16[576,128]{1,0:T(8,128)(2,1)S(1)}, bf16[576,128]{1,0:T(8,128)(2,1)S(1)}, u32[]{:S(2)}, u32[]{:S(2)}) collective-permute-start(bf16[576,128]{1,0:T(8,128)(2,1)S(1)} %collective-permute-done.15.refs_12_), channel_id=1, source_target_pairs={{0,28},{1,29},{2,30},{3,31},{4,0},{5,1},{6,2},{7,3},{8,4},{9,5},{1... | collective-permute-start | bytes 442376 | tf_op jit(solution)/shard_map/ppermute | solution.py:375
  34.9 2.8 %collective-permute-start.13 = (bf16[576,128]{1,0:T(8,128)(2,1)S(1)}, bf16[576,128]{1,0:T(8,128)(2,1)S(1)}, u32[]{:S(2)}, u32[]{:S(2)}) collective-permute-start(bf16[576,128]{1,0:T(8,128)(2,1)S(1)} %collective-permute-done.12.refs_11_), channel_id=1, source_target_pairs={{0,28},{1,29},{2,30},{3,31},{4,0},{5,1},{6,2},{7,3},{8,4},{9,5},{1... | collective-permute-start | bytes 442376 | tf_op jit(solution)/shard_map/ppermute | solution.py:375
  37.9 2.4 %collective-permute-done.9.refs_8_ = bf16[576,128]{1,0:T(8,128)(2,1)S(1)} collective-permute-done((bf16[576,128]{1,0:T(8,128)(2,1)S(1)}, bf16[576,128]{1,0:T(8,128)(2,1)S(1)}, u32[]{:S(2)}, u32[]{:S(2)}) %collective-permute-start.9) | collective-permute-done | bytes 147488 | tf_op jit(solution)/shard_map/ppermute | solution.py:375
  41.0 2.0 %collective-permute-start.18 = (bf16[32,64,128]{2,1,0:T(8,128)(2,1)}, bf16[32,64,128]{2,1,0:T(8,128)(2,1)S(1)}, u32[]{:S(2)}, u32[]{:S(2)}) collective-permute-start(bf16[32,64,128]{2,1,0:T(8,128)(2,1)} %get-tuple-element.28.co), channel_id=1, source_target_pairs={{0,1},{1,2},{2,3},{3,4},{4,5},{5,6},{6,7},{7,8},{8,9},{9,10},{10,1... | collective-permute-start | bytes 1572872 | tf_op jit(solution)/shard_map/ppermute | solution.py:379
  43.0 12.5 %collective-permute-start.19 = (bf16[32,64,128]{2,1,0:T(8,128)(2,1)}, bf16[32,64,128]{2,1,0:T(8,128)(2,1)S(1)}, u32[]{:S(2)}, u32[]{:S(2)}) collective-permute-start(bf16[32,64,128]{2,1,0:T(8,128)(2,1)} %get-tuple-element.28.co), channel_id=1, source_target_pairs={{1,0},{2,1},{3,2},{4,3},{5,4},{6,5},{7,6},{8,7},{9,8},{10,9},{11,1... | collective-permute-start | bytes 1572872 | tf_op jit(solution)/shard_map/ppermute | solution.py:379
  55.6 1.9 %collective-permute-start.20 = (bf16[32,64,128]{2,1,0:T(8,128)(2,1)}, bf16[32,64,128]{2,1,0:T(8,128)(2,1)S(1)}, u32[]{:S(2)}, u32[]{:S(2)}) collective-permute-start(bf16[32,64,128]{2,1,0:T(8,128)(2,1)} %get-tuple-element.30.ko), channel_id=1, source_target_pairs={{0,1},{1,2},{2,3},{3,4},{4,5},{5,6},{6,7},{7,8},{8,9},{9,10},{10,1... | collective-permute-start | bytes 1572872 | tf_op jit(solution)/shard_map/ppermute | solution.py:379
  57.5 7.0 %collective-permute-start.21 = (bf16[32,64,128]{2,1,0:T(8,128)(2,1)}, bf16[32,64,128]{2,1,0:T(8,128)(2,1)}, u32[]{:S(2)}, u32[]{:S(2)}) collective-permute-start(bf16[32,64,128]{2,1,0:T(8,128)(2,1)} %get-tuple-element.30.ko), channel_id=1, source_target_pairs={{1,0},{2,1},{3,2},{4,3},{5,4},{6,5},{7,6},{8,7},{9,8},{10,9},{11,1... | collective-permute-start | bytes 1572872 | tf_op jit(solution)/shard_map/ppermute | solution.py:379
  64.5 1.3 %collective-permute-start.17 = (bf16[1024,128]{1,0:T(8,128)(2,1)S(1)}, bf16[1024,128]{1,0:T(8,128)(2,1)S(1)}, u32[]{:S(2)}, u32[]{:S(2)}) collective-permute-start(bf16[1024,128]{1,0:T(8,128)(2,1)S(1)} %pick_tops.1.a), channel_id=1, source_target_pairs={{0,64},{1,65},{2,66},{3,67},{4,68},{5,69},{6,70},{7,71},{8,72},{9,... | collective-permute-start | bytes 786440 | tf_op jit(solution)/shard_map/ppermute | solution.py:375
  66.1 3.3 %collective-permute-start.22 = (bf16[1024,128]{1,0:T(8,128)(2,1)S(1)}, bf16[1024,128]{1,0:T(8,128)(2,1)}, u32[]{:S(2)}, u32[]{:S(2)}) collective-permute-start(bf16[1024,128]{1,0:T(8,128)(2,1)S(1)} %pick_tops.1.a), channel_id=1, source_target_pairs={{0,128},{1,129},{2,130},{3,131},{4,132},{5,133},{6,134},{7,135},{8... | collective-permute-start | bytes 786440 | tf_op jit(solution)/shard_map/ppermute | solution.py:375
  70.8 1.6 %copy-done = bf16[8,16,64,64]{3,2,1,0:T(8,128)(2,1)S(1)} copy-done((bf16[8,16,64,64]{3,2,1,0:T(8,128)(2,1)S(1)}, bf16[8,16,64,64]{3,2,1,0:T(8,128)(2,1)}, u32[]{:S(2)}) %copy-start) | copy-done | bytes 1048600
  73.1 5.5 %mid_far.1.far = f32[8,64,64]{2,1,0:T(8,128)S(1)} custom-call(s32[6]{0:T(128)S(1)} %stack.27.info, s32[8,16]{1,0:T(8,128)S(1)} %copy-done.7, bf16[8,16,64,64]{3,2,1,0:T(8,128)(2,1)S(1)} %copy-done, bf16[576,128]{1,0:T(8,128)(2,1)S(1)} %constant_dynamic-update-slice_fusion.refs_0_, bf16[576,128]{1,0:T(8,128)(2,1)S(1)} %constant_dynamic-update-slice_fusion.2.refs_1_, ...), custom_call_target="tpu_custom_call" | custom-call | flops 67108864 | bytes 6291456 | tf_op jit(solution)/shard_map/mid_far/pallas_call | solution.py:320
  78.6 9.0 %near.1 = (f32[64,64,64]{2,1,0:T(8,128)S(1)}, bf16[64,8,64,64]{3,2,1,0:T(8,128)(2,1)S(1)}, bf16[64,64,64]{2,1,0:T(8,128)(2,1)S(1)}, bf16[64,64,64]{2,1,0:T(8,128)(2,1)S(1)}) custom-call(s32[6]{0:T(128)} %copy-done.4, s32[8,64]{1,0:T(8,128)} %bitcast.9, s32[64]{0:T(128)} %cnt.1, bf16[32,64,128]{2,1,0:T(8,128)(2,1)} %copy-done.9, ...), custom_call_target="tpu_custom_call" | custom-call | flops 301989888 | bytes 25165824 | tf_op jit(solution)/shard_map/near/pallas_call | solution.py:149
  88.9 2.9 %collective-permute-start.24 = (bf16[4096,128]{1,0:T(8,128)(2,1)S(1)}, bf16[4096,128]{1,0:T(8,128)(2,1)S(1)}, u32[]{:S(2)}, u32[]{:S(2)}) collective-permute-start(bf16[4096,128]{1,0:T(8,128)(2,1)S(1)} %join.1.own), channel_id=1, source_target_pairs={{0,32},{1,33},{2,34},{3,35},{4,36},{5,37},{6,38},{7,39},{8,40},{9,... | collective-permute-start | bytes 3145736 | tf_op jit(solution)/shard_map/ppermute | solution.py:375
  92.4 7.8 %leaf_far.1.base = f32[64,64,64]{2,1,0:T(8,128)S(1)} custom-call(s32[6]{0:T(128)S(1)} %copy-done.5, s32[8,64]{1,0:T(8,128)S(1)} %bitcast.8, bf16[32,64,128]{2,1,0:T(8,128)(2,1)S(1)} %collective-permute-done.20.ku, bf16[32,64,128]{2,1,0:T(8,128)(2,1)S(1)} %copy-done.2, bf16[32,64,128]{2,1,0:T(8,128)(2,1)} %collective-permute-done.21.kd, ...), custom_call_target="tpu_custom_call" | custom-call | flops 301989888 | bytes 16777216 | tf_op jit(solution)/shard_map/leaf_far/pallas_call | solution.py:201
  101.4 1.4 %tail.1 = bf16[64,64,64]{2,1,0:T(8,128)(2,1)} custom-call(bf16[64,64]{1,0:T(8,128)(2,1)S(1)} %top_far.1.top_ref, f32[8,64,64]{2,1,0:T(8,128)S(1)} %mid_far.1.far, bf16[8,64,64]{2,1,0:T(8,128)(2,1)S(1)} %copy-done.3, f32[64,64,64]{2,1,0:T(8,128)S(1)} %leaf_far.1.base, bf16[64,64,64]{2,1,0:T(8,128)(2,1)S(1)} %get-tuple-element.38.both), custom_call_target="tpu_custom_call" | custom-call | flops 37748736 | bytes 6291456 | tf_op jit(solution)/shard_map/tail/pallas_call | solution.py:350
  (61 shorter events, 9.8 us)
Async XLA Ops:
  4.8 6.8 %collective-permute-start = (bf16[288,128]{1,0:T(8,128)(2,1)}, bf16[288,128]{1,0:T(8,128)(2,1)S(1)}, u32[]{:S(2)}, u32[]{:S(2)}) collective-permute-start(bf16[288,128]{1,0:T(8,128)(2,1)} %get-tuple-element.22), channel_id=1, source_target_pairs={{0,1},{1,2},{2,3},{3,0},{4,5},{5,6},{6,7},{7,4},{8,9},{9,10},{10,1... | collective-permute-start | bytes 221192 | tf_op jit(solution)/shard_map/ppermute | solution.py:375
  7.0 6.3 %collective-permute-start.1 = (bf16[288,128]{1,0:T(8,128)(2,1)}, bf16[288,128]{1,0:T(8,128)(2,1)S(1)}, u32[]{:S(2)}, u32[]{:S(2)}) collective-permute-start(bf16[288,128]{1,0:T(8,128)(2,1)} %get-tuple-element.22), channel_id=1, source_target_pairs={{0,2},{1,3},{2,0},{3,1},{4,6},{5,7},{6,4},{7,5},{8,10},{9,11},{10,... | collective-permute-start | bytes 221192 | tf_op jit(solution)/shard_map/ppermute | solution.py:375
  11.7 10.1 %collective-permute-start.3 = (bf16[576,128]{1,0:T(8,128)(2,1)S(1)}, bf16[576,128]{1,0:T(8,128)(2,1)S(1)}, u32[]{:S(2)}, u32[]{:S(2)}) collective-permute-start(bf16[576,128]{1,0:T(8,128)(2,1)S(1)} %constant_dynamic-update-slice_fusion.refs_0_), channel_id=1, source_target_pairs={{0,4},{1,5},{2,6},{3,7},{4,8},{5,9},{6,10},{7,11},{8,12},{9,13},{1... | collective-permute-start | bytes 442376 | tf_op jit(solution)/shard_map/ppermute | solution.py:375
  13.4 8.4 %collective-permute-start.10 = (bf16[576,128]{1,0:T(8,128)(2,1)S(1)}, bf16[576,128]{1,0:T(8,128)(2,1)S(1)}, u32[]{:S(2)}, u32[]{:S(2)}) collective-permute-start(bf16[576,128]{1,0:T(8,128)(2,1)S(1)} %constant_dynamic-update-slice_fusion.2.refs_1_), channel_id=1, source_target_pairs={{0,28},{1,29},{2,30},{3,31},{4,0},{5,1},{6,2},{7,3},{8,4},{9,5},{1... | collective-permute-start | bytes 442376 | tf_op jit(solution)/shard_map/ppermute | solution.py:375
  19.1 5.4 %collective-permute-start.4 = (bf16[576,128]{1,0:T(8,128)(2,1)S(1)}, bf16[576,128]{1,0:T(8,128)(2,1)S(1)}, u32[]{:S(2)}, u32[]{:S(2)}) collective-permute-start(bf16[576,128]{1,0:T(8,128)(2,1)S(1)} %constant_dynamic-update-slice_fusion.2.refs_1_), channel_id=1, source_target_pairs={{0,4},{1,5},{2,6},{3,7},{4,8},{5,9},{6,10},{7,11},{8,12},{9,13},{1... | collective-permute-start | bytes 442376 | tf_op jit(solution)/shard_map/ppermute | solution.py:375
  19.1 6.1 %collective-permute-start.14 = (bf16[576,128]{1,0:T(8,128)(2,1)S(1)}, bf16[576,128]{1,0:T(8,128)(2,1)S(1)}, u32[]{:S(2)}, u32[]{:S(2)}) collective-permute-start(bf16[576,128]{1,0:T(8,128)(2,1)S(1)} %constant_dynamic-update-slice_fusion.refs_0_), channel_id=1, source_target_pairs={{0,28},{1,29},{2,30},{3,31},{4,0},{5,1},{6,2},{7,3},{8,4},{9,5},{1... | collective-permute-start | bytes 442376 | tf_op jit(solution)/shard_map/ppermute | solution.py:375
  21.8 7.0 %collective-permute-start.5 = (bf16[576,128]{1,0:T(8,128)(2,1)S(1)}, bf16[576,128]{1,0:T(8,128)(2,1)S(1)}, u32[]{:S(2)}, u32[]{:S(2)}) collective-permute-start(bf16[576,128]{1,0:T(8,128)(2,1)S(1)} %collective-permute-done.3.refs_2_), channel_id=1, source_target_pairs={{0,4},{1,5},{2,6},{3,7},{4,8},{5,9},{6,10},{7,11},{8,12},{9,13},{1... | collective-permute-start | bytes 442376 | tf_op jit(solution)/shard_map/ppermute | solution.py:375
  21.8 7.0 %collective-permute-start.11 = (bf16[576,128]{1,0:T(8,128)(2,1)S(1)}, bf16[576,128]{1,0:T(8,128)(2,1)S(1)}, u32[]{:S(2)}, u32[]{:S(2)}) collective-permute-start(bf16[576,128]{1,0:T(8,128)(2,1)S(1)} %collective-permute-done.10.refs_15_), channel_id=1, source_target_pairs={{0,28},{1,29},{2,30},{3,31},{4,0},{5,1},{6,2},{7,3},{8,4},{9,5},{1... | collective-permute-start | bytes 442376 | tf_op jit(solution)/shard_map/ppermute | solution.py:375
  24.5 7.3 %collective-permute-start.6 = (bf16[576,128]{1,0:T(8,128)(2,1)S(1)}, bf16[576,128]{1,0:T(8,128)(2,1)S(1)}, u32[]{:S(2)}, u32[]{:S(2)}) collective-permute-start(bf16[576,128]{1,0:T(8,128)(2,1)S(1)} %collective-permute-done.4.refs_3_), channel_id=1, source_target_pairs={{0,4},{1,5},{2,6},{3,7},{4,8},{5,9},{6,10},{7,11},{8,12},{9,13},{1... | collective-permute-start | bytes 442376 | tf_op jit(solution)/shard_map/ppermute | solution.py:375
  25.3 6.6 %collective-permute-start.15 = (bf16[576,128]{1,0:T(8,128)(2,1)S(1)}, bf16[576,128]{1,0:T(8,128)(2,1)S(1)}, u32[]{:S(2)}, u32[]{:S(2)}) collective-permute-start(bf16[576,128]{1,0:T(8,128)(2,1)S(1)} %collective-permute-done.14.refs_14_), channel_id=1, source_target_pairs={{0,28},{1,29},{2,30},{3,31},{4,0},{5,1},{6,2},{7,3},{8,4},{9,5},{1... | collective-permute-start | bytes 442376 | tf_op jit(solution)/shard_map/ppermute | solution.py:375
  28.8 6.1 %collective-permute-start.7 = (bf16[576,128]{1,0:T(8,128)(2,1)S(1)}, bf16[576,128]{1,0:T(8,128)(2,1)S(1)}, u32[]{:S(2)}, u32[]{:S(2)}) collective-permute-start(bf16[576,128]{1,0:T(8,128)(2,1)S(1)} %collective-permute-done.5.refs_4_), channel_id=1, source_target_pairs={{0,4},{1,5},{2,6},{3,7},{4,8},{5,9},{6,10},{7,11},{8,12},{9,13},{1... | collective-permute-start | bytes 442376 | tf_op jit(solution)/shard_map/ppermute | solution.py:375
  28.8 6.1 %collective-permute-start.12 = (bf16[576,128]{1,0:T(8,128)(2,1)S(1)}, bf16[576,128]{1,0:T(8,128)(2,1)S(1)}, u32[]{:S(2)}, u32[]{:S(2)}) collective-permute-start(bf16[576,128]{1,0:T(8,128)(2,1)S(1)} %collective-permute-done.11.refs_13_), channel_id=1, source_target_pairs={{0,28},{1,29},{2,30},{3,31},{4,0},{5,1},{6,2},{7,3},{8,4},{9,5},{1... | collective-permute-start | bytes 442376 | tf_op jit(solution)/shard_map/ppermute | solution.py:375
  31.8 6.1 %collective-permute-start.8 = (bf16[576,128]{1,0:T(8,128)(2,1)S(1)}, bf16[576,128]{1,0:T(8,128)(2,1)S(1)}, u32[]{:S(2)}, u32[]{:S(2)}) collective-permute-start(bf16[576,128]{1,0:T(8,128)(2,1)S(1)} %collective-permute-done.6.refs_5_), channel_id=1, source_target_pairs={{0,4},{1,5},{2,6},{3,7},{4,8},{5,9},{6,10},{7,11},{8,12},{9,13},{1... | collective-permute-start | bytes 442376 | tf_op jit(solution)/shard_map/ppermute | solution.py:375
  31.8 6.1 %collective-permute-start.16 = (bf16[576,128]{1,0:T(8,128)(2,1)S(1)}, bf16[576,128]{1,0:T(8,128)(2,1)S(1)}, u32[]{:S(2)}, u32[]{:S(2)}) collective-permute-start(bf16[576,128]{1,0:T(8,128)(2,1)S(1)} %collective-permute-done.15.refs_12_), channel_id=1, source_target_pairs={{0,28},{1,29},{2,30},{3,31},{4,0},{5,1},{6,2},{7,3},{8,4},{9,5},{1... | collective-permute-start | bytes 442376 | tf_op jit(solution)/shard_map/ppermute | solution.py:375
  34.9 5.4 %collective-permute-start.9 = (bf16[576,128]{1,0:T(8,128)(2,1)S(1)}, bf16[576,128]{1,0:T(8,128)(2,1)S(1)}, u32[]{:S(2)}, u32[]{:S(2)}) collective-permute-start(bf16[576,128]{1,0:T(8,128)(2,1)S(1)} %collective-permute-done.7.refs_6_), channel_id=1, source_target_pairs={{0,4},{1,5},{2,6},{3,7},{4,8},{5,9},{6,10},{7,11},{8,12},{9,13},{1... | collective-permute-start | bytes 442376 | tf_op jit(solution)/shard_map/ppermute | solution.py:375
  34.9 5.4 %collective-permute-start.13 = (bf16[576,128]{1,0:T(8,128)(2,1)S(1)}, bf16[576,128]{1,0:T(8,128)(2,1)S(1)}, u32[]{:S(2)}, u32[]{:S(2)}) collective-permute-start(bf16[576,128]{1,0:T(8,128)(2,1)S(1)} %collective-permute-done.12.refs_11_), channel_id=1, source_target_pairs={{0,28},{1,29},{2,30},{3,31},{4,0},{5,1},{6,2},{7,3},{8,4},{9,5},{1... | collective-permute-start | bytes 442376 | tf_op jit(solution)/shard_map/ppermute | solution.py:375
  41.0 25.1 %collective-permute-start.18 = (bf16[32,64,128]{2,1,0:T(8,128)(2,1)}, bf16[32,64,128]{2,1,0:T(8,128)(2,1)S(1)}, u32[]{:S(2)}, u32[]{:S(2)}) collective-permute-start(bf16[32,64,128]{2,1,0:T(8,128)(2,1)} %get-tuple-element.28.co), channel_id=1, source_target_pairs={{0,1},{1,2},{2,3},{3,4},{4,5},{5,6},{6,7},{7,8},{8,9},{9,10},{10,1... | collective-permute-start | bytes 1572872 | tf_op jit(solution)/shard_map/ppermute | solution.py:379
  43.0 26.3 %collective-permute-start.19 = (bf16[32,64,128]{2,1,0:T(8,128)(2,1)}, bf16[32,64,128]{2,1,0:T(8,128)(2,1)S(1)}, u32[]{:S(2)}, u32[]{:S(2)}) collective-permute-start(bf16[32,64,128]{2,1,0:T(8,128)(2,1)} %get-tuple-element.28.co), channel_id=1, source_target_pairs={{1,0},{2,1},{3,2},{4,3},{5,4},{6,5},{7,6},{8,7},{9,8},{10,9},{11,1... | collective-permute-start | bytes 1572872 | tf_op jit(solution)/shard_map/ppermute | solution.py:379
  55.6 32.1 %collective-permute-start.20 = (bf16[32,64,128]{2,1,0:T(8,128)(2,1)}, bf16[32,64,128]{2,1,0:T(8,128)(2,1)S(1)}, u32[]{:S(2)}, u32[]{:S(2)}) collective-permute-start(bf16[32,64,128]{2,1,0:T(8,128)(2,1)} %get-tuple-element.30.ko), channel_id=1, source_target_pairs={{0,1},{1,2},{2,3},{3,4},{4,5},{5,6},{6,7},{7,8},{8,9},{9,10},{10,1... | collective-permute-start | bytes 1572872 | tf_op jit(solution)/shard_map/ppermute | solution.py:379
  57.5 30.2 %collective-permute-start.21 = (bf16[32,64,128]{2,1,0:T(8,128)(2,1)}, bf16[32,64,128]{2,1,0:T(8,128)(2,1)}, u32[]{:S(2)}, u32[]{:S(2)}) collective-permute-start(bf16[32,64,128]{2,1,0:T(8,128)(2,1)} %get-tuple-element.30.ko), channel_id=1, source_target_pairs={{1,0},{2,1},{3,2},{4,3},{5,4},{6,5},{7,6},{8,7},{9,8},{10,9},{11,1... | collective-permute-start | bytes 1572872 | tf_op jit(solution)/shard_map/ppermute | solution.py:379
  64.5 23.2 %collective-permute-start.17 = (bf16[1024,128]{1,0:T(8,128)(2,1)S(1)}, bf16[1024,128]{1,0:T(8,128)(2,1)S(1)}, u32[]{:S(2)}, u32[]{:S(2)}) collective-permute-start(bf16[1024,128]{1,0:T(8,128)(2,1)S(1)} %pick_tops.1.a), channel_id=1, source_target_pairs={{0,64},{1,65},{2,66},{3,67},{4,68},{5,69},{6,70},{7,71},{8,72},{9,... | collective-permute-start | bytes 786440 | tf_op jit(solution)/shard_map/ppermute | solution.py:375
  66.1 21.6 %collective-permute-start.22 = (bf16[1024,128]{1,0:T(8,128)(2,1)S(1)}, bf16[1024,128]{1,0:T(8,128)(2,1)}, u32[]{:S(2)}, u32[]{:S(2)}) collective-permute-start(bf16[1024,128]{1,0:T(8,128)(2,1)S(1)} %pick_tops.1.a), channel_id=1, source_target_pairs={{0,128},{1,129},{2,130},{3,131},{4,132},{5,133},{6,134},{7,135},{8... | collective-permute-start | bytes 786440 | tf_op jit(solution)/shard_map/ppermute | solution.py:375
  70.1 17.6 %collective-permute-start.23 = (bf16[1024,128]{1,0:T(8,128)(2,1)S(1)}, bf16[1024,128]{1,0:T(8,128)(2,1)}, u32[]{:S(2)}, u32[]{:S(2)}) collective-permute-start(bf16[1024,128]{1,0:T(8,128)(2,1)S(1)} %pick_tops.1.a), channel_id=1, source_target_pairs={{0,192},{1,193},{2,194},{3,195},{4,196},{5,197},{6,198},{7,199},{8... | collective-permute-start | bytes 786440 | tf_op jit(solution)/shard_map/ppermute | solution.py:375
  88.9 11.4 %collective-permute-start.24 = (bf16[4096,128]{1,0:T(8,128)(2,1)S(1)}, bf16[4096,128]{1,0:T(8,128)(2,1)S(1)}, u32[]{:S(2)}, u32[]{:S(2)}) collective-permute-start(bf16[4096,128]{1,0:T(8,128)(2,1)S(1)} %join.1.own), channel_id=1, source_target_pairs={{0,32},{1,33},{2,34},{3,35},{4,36},{5,37},{6,38},{7,39},{8,40},{9,... | collective-permute-start | bytes 3145736 | tf_op jit(solution)/shard_map/ppermute | solution.py:375
  (12 other events, 76.7 us)
